TPU v7x, 256 devices: a whole 4x4x8 slice. The times are simulated.
256 devices in a mesh: blk: 16 (over y_lo, x, core), width: 16 (over y_hi, z).
Axes of the slice: x: 4, y: 4 (y_hi: 2, y_lo: 2; y = y_hi * 2 + y_lo), z: 8, core: 2. Of those that a mesh axis runs over, the one named last changes fastest.
Arguments:
- inputs: bfloat16 [16, 128, 2048], P('blk', None, 'width'), may hold values from -6 to 6
- encoder: bfloat16 [16, 2048, 4096], P('blk', 'width'), may hold values from -0.125 to 0.125
- enc_bias: float32 [16, 4096], P('blk'), may hold values from -3 to 3
- active_blocks: int32 [16, 128, 32], P('blk'), may hold values 0 or 1
- near_decoders: bfloat16 [16, 8, 4096, 2048], P('blk', None, None, 'width'), may hold values from -0.09375 to 0.09375
- far_decoders: bfloat16 [16, 2048, 2048], P('blk', None, 'width'), may hold values from -0.09375 to 0.09375
- targets: bfloat16 [16, 128, 2048], P('blk', None, 'width'), may hold values from -6 to 6
Outputs:
- reconstruction: float32 [16, 128, 2048], P('blk', None, 'width')
- grad_encoder: bfloat16 [16, 2048, 4096], P('blk', 'width')
- grad_bias: float32 [16, 4096], P('blk')
All inputs are finite; a program needn't handle non-finite values. No bound on the sum of `active_blocks` on one device may be relied on, other than what follows from the above.
Results may differ from a plain program's by a relative error of at most 0.011.
Values may be sent and summed in bfloat16 or wider, within the bound.
No kernel may reach another device: no remote copies, remote signals or barrier semaphores. Data moves between devices by JAX's collectives and lax.ppermute only.
A program may use at most 128 MiB of HBM per device.

v0:
```python
import jax
import jax.numpy as jnp
from jax import lax
from jax.sharding import PartitionSpec as P

FBLK = 128


def cut_along(shard, dim, count):
    shape = shard.shape
    parts = shard.reshape(*shape[:dim], count, shape[dim] // count, *shape[dim + 1 :])
    return jnp.moveaxis(parts, dim, 0)


def sent_and_summed(shard, axis, dim):
    count = lax.axis_size(axis)
    parts = lax.all_to_all(cut_along(shard, dim, count), axis, 0, 0, tiled=True)
    return jnp.sum(parts.astype(jnp.float32), axis=0)


def laid_out(parts, dim):
    shape = list(parts.shape[1:])
    shape[dim] *= parts.shape[0]
    return jnp.moveaxis(parts, 0, dim).reshape(shape)


def sent_to_all(shard, axis):
    count = lax.axis_size(axis)
    return lax.all_to_all(
        jnp.broadcast_to(shard[None], (count, *shard.shape)), axis, 0, 0, tiled=True
    )


def collect(shard, axis, dim):
    return laid_out(sent_to_all(shard, axis), dim)


def shifted(block, axis, distance):
    devices = range(lax.axis_size(axis))
    route = [(i - distance, i) for i in devices if i - distance in devices]
    return lax.ppermute(block, axis, route)


def sent_and_summed_2(shard, axis, dim):
    parts = cut_along(shard, dim, lax.axis_size(axis))
    arrived = lax.all_to_all(parts, axis, split_axis=0, concat_axis=0, tiled=True)
    return arrived.sum(axis=0)


def expand_mask(blocks):
    token_count, block_count = blocks.shape
    spread = jnp.broadcast_to(
        blocks.astype(jnp.float32)[:, :, None], (token_count, block_count, FBLK)
    )
    return spread.reshape(token_count, block_count * FBLK)


def forward_product(activations, weights):
    return jnp.dot(activations, weights, preferred_element_type=jnp.float32)


def backward_product(grads, weights):
    return lax.dot_general(
        grads, weights, (((1,), (1,)), ((), ())), preferred_element_type=jnp.float32
    )


def pick_row(stacked, position):
    return lax.dynamic_index_in_dim(stacked, position, 0, keepdims=False)


def on_device(inputs, encoder, enc_bias, active_blocks, near_decoders, far_decoders, targets):
    layers = lax.axis_size("blk")
    cycle_index = lax.axis_index("blk")
    near_count = layers // 2
    half_rows = far_decoders.shape[1]
    local_in = inputs[0]
    tok_rows = local_in.shape[0]
    width_cols = targets.shape[2]
    feature_count = encoder.shape[2]
    mask_full = expand_mask(active_blocks[0])
    partial_pre = jnp.dot(local_in, encoder[0], preferred_element_type=jnp.float32)
    shard_pre = sent_and_summed(partial_pre.astype(jnp.bfloat16), "width", 1)
    columns = shard_pre.shape[1]
    start_col = lax.axis_index("width") * columns
    mask_part = lax.dynamic_slice_in_dim(mask_full, start_col, columns, 1)
    bias_part = lax.dynamic_slice_in_dim(enc_bias[0], start_col, columns, 0)
    act_part = (mask_part * (shard_pre + bias_part)).astype(jnp.bfloat16)
    activations = collect(act_part, "width", 1)
    empty_rows = jnp.zeros((tok_rows, width_cols), jnp.float32)
    empty_grad = jnp.zeros((tok_rows, feature_count), jnp.float32)
    buffer = jnp.zeros((layers, tok_rows, width_cols), jnp.float32)
    buffer = buffer.at[cycle_index].add(forward_product(activations, near_decoders[0, 0]))
    moved_slots = []
    for offset in range(1, near_count):
        inside = cycle_index >= offset
        wrap_row = (cycle_index - offset + layers) % layers
        slot = near_decoders[0, offset]
        arrived = shifted(slot, "blk", -offset)
        moved_slots.append(arrived)
        own_term = lax.cond(inside, lambda: empty_rows, lambda: forward_product(activations, slot))
        buffer = buffer.at[wrap_row].add(own_term)
        moved_term = lax.cond(
            cycle_index < layers - offset,
            lambda: forward_product(activations, arrived),
            lambda: empty_rows,
        )
        buffer = buffer.at[(cycle_index + offset) % layers].add(moved_term)
    arrived_high = shifted(activations[:, half_rows:], "blk", near_count)
    upper_half = cycle_index >= near_count
    far_source = jnp.where(upper_half, arrived_high, activations[:, :half_rows])
    far_target = cycle_index % near_count + near_count
    buffer = buffer.at[far_target].add(forward_product(far_source, far_decoders[0]))
    reconstruction = sent_and_summed_2(buffer, "blk", 0)
    out_grad = (reconstruction - targets.astype(jnp.float32)).astype(jnp.bfloat16)
    all_grads = collect(out_grad, "blk", 0)
    own_grad = backward_product(pick_row(all_grads, cycle_index), near_decoders[0, 0])
    for offset in range(1, near_count):
        inside = cycle_index >= offset
        wrap_row = (cycle_index - offset + layers) % layers
        slot = near_decoders[0, offset]
        arrived = moved_slots[offset - 1]
        own_term = lax.cond(
            inside,
            lambda: empty_grad,
            lambda: backward_product(pick_row(all_grads, wrap_row), slot),
        )
        moved_row = (cycle_index + offset) % layers
        moved_term = lax.cond(
            cycle_index < layers - offset,
            lambda: backward_product(pick_row(all_grads, moved_row), arrived),
            lambda: empty_grad,
        )
        own_grad = own_grad + own_term + moved_term
    far_grad = backward_product(pick_row(all_grads, far_target), far_decoders[0])
    returned = shifted(
        jnp.where(upper_half, far_grad, 0.0).astype(jnp.bfloat16), "blk", -near_count
    ).astype(jnp.float32)
    lower_add = jnp.where(upper_half, 0.0, far_grad)
    own_grad = own_grad + jnp.concatenate([lower_add, returned], axis=1)
    grad_part = sent_and_summed(own_grad.astype(jnp.bfloat16), "width", 1)
    columns = grad_part.shape[1]
    start_col = lax.axis_index("width") * columns
    mask_slice = lax.dynamic_slice_in_dim(mask_full, start_col, columns, 1)
    pre_grad = collect((mask_slice * grad_part).astype(jnp.bfloat16), "width", 1)
    enc_grad = lax.dot_general(
        local_in, pre_grad, (((0,), (0,)), ((), ())), preferred_element_type=jnp.float32
    )
    bias_grad = jnp.sum(pre_grad.astype(jnp.float32), axis=0)
    return (reconstruction, enc_grad.astype(jnp.bfloat16)[None], bias_grad[None])


def solution(mesh):
    return jax.shard_map(
        on_device,
        mesh=mesh,
        in_specs=(
            P("blk", None, "width"),
            P("blk", "width", None),
            P("blk", None),
            P("blk", None, None),
            P("blk", None, None, "width"),
            P("blk", None, "width"),
            P("blk", None, "width"),
        ),
        out_specs=(P("blk", None, "width"), P("blk", "width", None), P("blk", None)),
        check_vma=False,
    )
```

profile of v0, /device:TPU:32, one launch (start us, length us, event | category | flops | bytes accessed | tf_op | source)
XLA Modules:
  0.0 414.6 jit_solution(7643583291903187713)
XLA Ops:
  4.1 11.2 %all-to-all-start = ((bf16[16,128,256]{2,1,0:T(8,128)(2,1)}), bf16[16,128,256]{2,1,0:T(8,128)(2,1)S(1)}, u32[]{:S(2)}, u32[]{:S(2)}) async-start(bf16[16,128,256]{2,1,0:T(8,128)(2,1)} %bitcast.233), calls=%async_computation | async-start | bytes 2097152 | tf_op jit(solution)/shard_map/all_to_all | solution.py:17
  19.7 23.4 %all-to-all-done = bf16[16,128,256]{2,1,0:T(8,128)(2,1)S(1)} async-done(((bf16[16,128,256]{2,1,0:T(8,128)(2,1)}), bf16[16,128,256]{2,1,0:T(8,128)(2,1)S(1)}, u32[]{:S(2)}, u32[]{:S(2)}) %all-to-all-start) | async-done | bytes 1048608 | tf_op jit(solution)/shard_map/all_to_all | solution.py:17
  45.3 5.2 %all-to-all-start.1 = ((bf16[16,128,256]{2,1,0:T(8,128)(2,1)}), bf16[16,128,256]{2,1,0:T(8,128)(2,1)S(1)}, u32[]{:S(2)}, u32[]{:S(2)}) async-start(bf16[16,128,256]{2,1,0:T(8,128)(2,1)} %broadcast_in_dim.70), calls=%async_computation.1 | async-start | bytes 2097152 | tf_op jit(solution)/shard_map/all_to_all | solution.py:29
  50.5 5.5 %slice_bitcast_fusion = (bf16[4096,128]{1,0:T(8,128)(2,1)S(1)}, bf16[4096,128]{1,0:T(8,128)(2,1)}, bf16[4096,128]{1,0:T(8,128)(2,1)}, bf16[4096,128]{1,0:T(8,128...) fusion(bf16[1,8,4096,128]{3,2,1,0:T(8,128)(2,1)} %param.99), kind=kLoop, calls=%fused_computation.94 | loop fusion | bytes 14680064 | tf_op jit(solution)/shard_map/squeeze | solution.py:98
  66.0 12.4 %all-to-all-done.1 = bf16[16,128,256]{2,1,0:T(8,128)(2,1)S(1)} async-done(((bf16[16,128,256]{2,1,0:T(8,128)(2,1)}), bf16[16,128,256]{2,1,0:T(8,128)(2,1)S(1)}, u32[]{:S(2)}, u32[]{:S(2)}) %all-to-all-start.1) | async-done | bytes 1048608 | tf_op jit(solution)/shard_map/all_to_all | solution.py:29
  97.5 51.7 %collective-permute-start.7 = (bf16[128,2048]{1,0:T(8,128)(2,1)}, bf16[128,2048]{1,0:T(8,128)(2,1)}, u32[]{:S(2)}, u32[]{:S(2)}) collective-permute-start(bf16[128,2048]{1,0:T(8,128)(2,1)} %slice.352), channel_id=1, source_target_pairs={{0,128},{16,144},{32,160},{48,176},{64,192},{80,208},{96,224},{112... | collective-permute-start | bytes 1572872 | tf_op jit(solution)/shard_map/ppermute | solution.py:41
  196.4 71.6 %all_to_all.30 = f32[16,1,128,128]{3,2,1,0:T(8,128)S(1)} all-to-all(f32[16,1,128,128]{3,2,1,0:T(8,128)S(1)} %bitcast.255), channel_id=1, replica_groups=mesh['blk'=16,'width'=16] {'blk'}, dimensions={0} | all-to-all | bytes 2097152 | tf_op jit(solution)/shard_map/all_to_all | solution.py:46
  269.0 3.6 all-to-all-start.3
  272.6 10.8 %all-to-all-done.3 = bf16[16,1,128,128]{3,2,1,0:T(8,128)(2,1)S(1)} async-done(((bf16[16,1,128,128]{3,2,1,0:T(8,128)(2,1)}), bf16[16,1,128,128]{3,2,1,0:T(8,128)(2,1)S(1)}, u32[]{:S(2)}, u32[]{:S(2)}) %all-to-all-start.3) | async-done | bytes 524320 | tf_op jit(solution)/shard_map/all_to_all | solution.py:29
  287.7 3.1 conditional.42
  287.7 3.0 fusion
  290.7 3.7 convolution_add_fusion
  294.4 3.0 conditional.43
  294.4 3.0 fusion.4
  300.4 3.1 conditional.45
  300.4 3.1 fusion.12
  303.5 3.0 conditional.46
  303.5 3.0 fusion.16
  306.5 3.1 conditional.47
  306.5 3.1 fusion.20
  309.6 3.1 conditional.48
  309.6 3.1 fusion.24
  312.7 3.0 conditional.49
  312.7 3.0 fusion.28
  315.7 3.1 conditional.50
  315.7 3.1 fusion.32
  324.3 3.0 conditional.53
  329.8 3.0 conditional.55
  329.8 3.0 fusion.52
  334.6 9.9 %fusion.57 = bf16[128,4096]{1,0:T(8,128)(2,1)S(1)} fusion(f32[128,2048]{1,0:T(8,128)S(1)} %convert_element_type.128, f32[128,2048]{1,0:T(8,128)S(1)} %broadcast_select_fusion, f32[128,4096]{1,0:T(8,128)} %get-tuple-element.572, f32[128,4096]{1,0:T(8,128)} %get-tuple-element.571, f32[128,4096]{1,0:T(8,128)} %get-tuple-element.570, ...), kind=kLoop, calls=%fused_computation.76 | loop fusion | flops 8388608 | bytes 32505856 | tf_op jit(solution)/shard_map/convert_element_type | solution.py:141
  344.6 34.5 %all_to_all.31 = bf16[16,128,256]{2,1,0:T(8,128)(2,1)S(1)} all-to-all(bf16[16,128,256]{2,1,0:T(8,128)(2,1)S(1)} %bitcast.256), channel_id=1, replica_groups=mesh['blk'=16,'width'=16] {'width'}, dimensions={0} | all-to-all | bytes 2097152 | tf_op jit(solution)/shard_map/all_to_all | solution.py:17
  380.5 31.4 %all_to_all.32 = bf16[16,128,256]{1,2,0:T(8,128)(2,1)S(1)} all-to-all(bf16[16,128,256]{1,2,0:T(8,128)(2,1)S(1)} %broadcast_in_dim.78), channel_id=1, replica_groups=mesh['blk'=16,'width'=16] {'width'}, dimensions={0} | all-to-all | bytes 2097152 | tf_op jit(solution)/shard_map/all_to_all | solution.py:29
  (129 shorter events, 145.7 us)
Async XLA Ops:
  0.6 1.2 copy-start
  3.0 12.3 %copy-start.11 = (s32[1,128,32]{1,2,0:T(8,128)S(1)}, s32[1,128,32]{1,2,0:T(8,128)}, u32[]{:S(2)}) copy-start(s32[1,128,32]{1,2,0:T(8,128)} %param.98) | copy-start | bytes 49156
  4.1 39.0 %all-to-all-start = ((bf16[16,128,256]{2,1,0:T(8,128)(2,1)}), bf16[16,128,256]{2,1,0:T(8,128)(2,1)S(1)}, u32[]{:S(2)}, u32[]{:S(2)}) async-start(bf16[16,128,256]{2,1,0:T(8,128)(2,1)} %bitcast.233), calls=%async_computation | async-start | bytes 2097152 | tf_op jit(solution)/shard_map/all_to_all | solution.py:17
  45.3 33.1 %all-to-all-start.1 = ((bf16[16,128,256]{2,1,0:T(8,128)(2,1)}), bf16[16,128,256]{2,1,0:T(8,128)(2,1)S(1)}, u32[]{:S(2)}, u32[]{:S(2)}) async-start(bf16[16,128,256]{2,1,0:T(8,128)(2,1)} %broadcast_in_dim.70), calls=%async_computation.1 | async-start | bytes 2097152 | tf_op jit(solution)/shard_map/all_to_all | solution.py:29
  50.5 12.3 %copy-start.12 = (s32[3]{0:T(128)S(1)}, s32[3]{0:T(128)}, u32[]{:S(2)}) copy-start(s32[3]{0:T(128)} %constant.584.clone.1) | copy-start | bytes 40
  56.0 34.3 %collective-permute-start.4 = (bf16[4096,128]{1,0:T(8,128)(2,1)}, bf16[4096,128]{1,0:T(8,128)(2,1)}, u32[]{:S(2)}, u32[]{:S(2)}) collective-permute-start(bf16[4096,128]{1,0:T(8,128)(2,1)} %get-tuple-element.529), channel_id=1, source_target_pairs={{80,0},{96,16},{112,32},{128,48},{144,64},{160,80},{176,96},{192,1... | collective-permute-start | bytes 3145736 | tf_op jit(solution)/shard_map/ppermute | solution.py:41
  57.3 36.6 %collective-permute-start.3 = (bf16[4096,128]{1,0:T(8,128)(2,1)}, bf16[4096,128]{1,0:T(8,128)(2,1)}, u32[]{:S(2)}, u32[]{:S(2)}) collective-permute-start(bf16[4096,128]{1,0:T(8,128)(2,1)} %get-tuple-element.530), channel_id=1, source_target_pairs={{64,0},{80,16},{96,32},{112,48},{128,64},{144,80},{160,96},{176,11... | collective-permute-start | bytes 3145736 | tf_op jit(solution)/shard_map/ppermute | solution.py:41
  58.6 38.9 %collective-permute-start.2 = (bf16[4096,128]{1,0:T(8,128)(2,1)}, bf16[4096,128]{1,0:T(8,128)(2,1)}, u32[]{:S(2)}, u32[]{:S(2)}) collective-permute-start(bf16[4096,128]{1,0:T(8,128)(2,1)} %get-tuple-element.531), channel_id=1, source_target_pairs={{48,0},{64,16},{80,32},{96,48},{112,64},{128,80},{144,96},{160,112... | collective-permute-start | bytes 3145736 | tf_op jit(solution)/shard_map/ppermute | solution.py:41
  59.9 91.6 %collective-permute-start.1 = (bf16[4096,128]{1,0:T(8,128)(2,1)}, bf16[4096,128]{1,0:T(8,128)(2,1)}, u32[]{:S(2)}, u32[]{:S(2)}) collective-permute-start(bf16[4096,128]{1,0:T(8,128)(2,1)} %get-tuple-element.532), channel_id=1, source_target_pairs={{32,0},{48,16},{64,32},{80,48},{96,64},{112,80},{128,96},{144,112}... | collective-permute-start | bytes 3145736 | tf_op jit(solution)/shard_map/ppermute | solution.py:41
  61.2 98.6 %collective-permute-start = (bf16[4096,128]{1,0:T(8,128)(2,1)}, bf16[4096,128]{1,0:T(8,128)(2,1)}, u32[]{:S(2)}, u32[]{:S(2)}) collective-permute-start(bf16[4096,128]{1,0:T(8,128)(2,1)} %get-tuple-element.533), channel_id=1, source_target_pairs={{16,0},{32,16},{48,32},{64,48},{80,64},{96,80},{112,96},{128,112},... | collective-permute-start | bytes 3145736 | tf_op jit(solution)/shard_map/ppermute | solution.py:41
  78.4 1.0 copy-start.3
  90.3 84.4 %collective-permute-start.5 = (bf16[4096,128]{1,0:T(8,128)(2,1)S(1)}, bf16[4096,128]{1,0:T(8,128)(2,1)}, u32[]{:S(2)}, u32[]{:S(2)}) collective-permute-start(bf16[4096,128]{1,0:T(8,128)(2,1)S(1)} %get-tuple-element.534), channel_id=1, source_target_pairs={{96,0},{112,16},{128,32},{144,48},{160,64},{176,80},{192,96},{208,... | collective-permute-start | bytes 3145736 | tf_op jit(solution)/shard_map/ppermute | solution.py:41
  93.9 93.5 %collective-permute-start.6 = (bf16[4096,128]{1,0:T(8,128)(2,1)S(1)}, bf16[4096,128]{1,0:T(8,128)(2,1)}, u32[]{:S(2)}, u32[]{:S(2)}) collective-permute-start(bf16[4096,128]{1,0:T(8,128)(2,1)S(1)} %get-tuple-element.528), channel_id=1, source_target_pairs={{112,0},{128,16},{144,32},{160,48},{176,64},{192,80},{208,96},{224... | collective-permute-start | bytes 3145736 | tf_op jit(solution)/shard_map/ppermute | solution.py:41
  97.5 97.1 %collective-permute-start.7 = (bf16[128,2048]{1,0:T(8,128)(2,1)}, bf16[128,2048]{1,0:T(8,128)(2,1)}, u32[]{:S(2)}, u32[]{:S(2)}) collective-permute-start(bf16[128,2048]{1,0:T(8,128)(2,1)} %slice.352), channel_id=1, source_target_pairs={{0,128},{16,144},{32,160},{48,176},{64,192},{80,208},{96,224},{112... | collective-permute-start | bytes 1572872 | tf_op jit(solution)/shard_map/ppermute | solution.py:41
  162.1 18.6 %copy-start.7 = (f32[1,128,128]{2,1,0:T(8,128)S(1)}, f32[1,128,128]{2,1,0:T(8,128)}, u32[]{:S(2)}) copy-start(f32[1,128,128]{2,1,0:T(8,128)} %get-tuple-element.554) | copy-start | bytes 196612
  166.4 10.1 %copy-start.8 = (f32[1,128,128]{2,1,0:T(8,128)S(1)}, f32[1,128,128]{2,1,0:T(8,128)}, u32[]{:S(2)}) copy-start(f32[1,128,128]{2,1,0:T(8,128)} %get-tuple-element.552) | copy-start | bytes 196612
  189.2 5.4 %copy-start.5 = (bf16[1,2048,128]{2,1,0:T(8,128)(2,1)S(1)}, bf16[1,2048,128]{2,1,0:T(8,128)(2,1)}, u32[]{:S(2)}) copy-start(bf16[1,2048,128]{2,1,0:T(8,128)(2,1)} %param.100) | copy-start | bytes 1572868
  194.6 73.5 %copy-start.10 = (bf16[1,128,128]{2,1,0:T(8,128)(2,1)S(1)}, bf16[1,128,128]{2,1,0:T(8,128)(2,1)}, u32[]{:S(2)}) copy-start(bf16[1,128,128]{2,1,0:T(8,128)(2,1)} %param.101) | copy-start | bytes 98308
  268.1 19.6 %copy-start.6 = (f32[128,128]{1,0:T(8,128)}, f32[128,128]{1,0:T(8,128)S(1)}, u32[]{:S(2)}) copy-start(f32[128,128]{1,0:T(8,128)S(1)} %reduce_sum.39) | copy-start | bytes 196612
  269.0 14.4 %all-to-all-start.3 = ((bf16[16,1,128,128]{3,2,1,0:T(8,128)(2,1)}), bf16[16,1,128,128]{3,2,1,0:T(8,128)(2,1)S(1)}, u32[]{:S(2)}, u32[]{:S(2)}) async-start(bf16[16,1,128,128]{3,2,1,0:T(8,128)(2,1)} %broadcast_in_dim.74), calls=%async_computation.3 | async-start | bytes 1048576 | tf_op jit(solution)/shard_map/all_to_all | solution.py:29
  283.4 0.8 copy-start.4
  286.4 46.6 %collective-permute-start.8 = (bf16[128,2048]{1,0:T(8,128)(2,1)}, bf16[128,2048]{1,0:T(8,128)(2,1)}, u32[]{:S(2)}, u32[]{:S(2)}) collective-permute-start(bf16[128,2048]{1,0:T(8,128)(2,1)} %get-tuple-element.543), channel_id=1, source_target_pairs={{128,0},{144,16},{160,32},{176,48},{192,64},{208,80},{224,96},{240... | collective-permute-start | bytes 1572872 | tf_op jit(solution)/shard_map/ppermute | solution.py:41
  332.9 1.7 copy-start.2
  380.2 32.6 %copy-start.9 = (bf16[1,128,128]{2,1,0:T(8,128)(2,1)S(1)}, bf16[1,128,128]{2,1,0:T(8,128)(2,1)}, u32[]{:S(2)}) copy-start(bf16[1,128,128]{2,1,0:T(8,128)(2,1)} %param.95) | copy-start | bytes 98308
  412.8 1.7 copy-start.1
where the time goes:
time: 417 us; the launch traced here: 415 us
  blocking collectives  137 us (33%)
  starting transfers between devices  82 us (20%)
  matrix products  77.3 us (19%)
  waiting for transfers between devices  46.6 us (11%)
  other arithmetic  46.2 us (11%)
  local copies, waits for them, and re-layouts  23.2 us (6%)
    all_to_all x1, blocking collectives, sent_and_summed_2(): lax.all_to_all(parts, axis, split_axis=0, concat_axis=0, tiled=True)  71.6 us
    ppermute x9, starting transfers between devices, shifted(): return lax.ppermute(block, axis, route)  62 us
    dot_general x16, matrix products, backward_product(): lax.dot_general(grads, weights, (((1,), (1,)), ((), ())), preferred_eleme...  47.3 us
    all_to_all x1, blocking collectives, sent_and_summed(): parts = lax.all_to_all(cut_along(shard, dim, count), axis, 0, 0, tiled=True)  34.5 us
    all_to_all x1, blocking collectives, sent_to_all(): lax.all_to_all(jnp.broadcast_to(shard[None], (count, *shard.shape)), axis...  31.4 us
    dot_general x16, matrix products, forward_product(): return jnp.dot(activations, weights, preferred_element_type=jnp.float32)  28.4 us
    all_to_all x1, waiting for transfers between devices, sent_and_summed(): parts = lax.all_to_all(cut_along(shard, dim, count), axis, 0, 0, tiled=True)  23.4 us
    all_to_all x2, waiting for transfers between devices, sent_to_all(): lax.all_to_all(jnp.broadcast_to(shard[None], (count, *shard.shape)), axis...  23.2 us
  transfers between devices with their start and end apart: 12, of which 3 were waited for; matrix products, arithmetic and copies ran while one was open for 29% of the time, Pallas kernels for 0%

commit v1 on v0

v1 whole, which is shorter than its diff:
```python
import functools

import jax
import jax.numpy as jnp
from jax import lax
from jax.experimental import pallas as pl
from jax.experimental.pallas import tpu as pltpu
from jax.sharding import PartitionSpec as P

FBLK = 128
BF16 = jnp.bfloat16
F32 = jnp.float32
SMEM = pltpu.MemorySpace.SMEM
VMEM_LIMIT = 40 * 1024 * 1024


def exchange(parts, axis):
    return lax.all_to_all(parts, axis, 0, 0, tiled=True)


def shifted_down(block, distance, lowest=0):
    count = lax.axis_size("blk")
    route = [(i, i - distance) for i in range(count) if i - distance >= lowest]
    return lax.ppermute(block, "blk", route)


def pre_kernel(in_ref, enc_ref, out_ref):
    columns = out_ref.shape[2]
    product = jnp.dot(in_ref[...], enc_ref[...], preferred_element_type=F32)
    for part in range(out_ref.shape[0]):
        out_ref[part] = product[:, part * columns : (part + 1) * columns].astype(BF16)


def pre_parts(local_in, encoder, parts):
    tokens, rows = local_in.shape
    features = encoder.shape[1]
    columns = features // parts
    step = 4
    return pl.pallas_call(
        pre_kernel,
        grid=(parts // step,),
        in_specs=[
            pl.BlockSpec((tokens, rows), lambda c: (0, 0)),
            pl.BlockSpec((rows, step * columns), lambda c: (0, c)),
        ],
        out_specs=pl.BlockSpec((step, tokens, columns), lambda c: (c, 0, 0)),
        out_shape=jax.ShapeDtypeStruct((parts, tokens, columns), BF16),
        name="pre_parts",
    )(local_in, encoder)


def masked_sum_kernel(parts_ref, bias_ref, blocks_ref, out_ref):
    count, tokens, columns = parts_ref.shape
    total = parts_ref[0].astype(F32)
    for part in range(1, count):
        total = total + parts_ref[part].astype(F32)
    total = total + bias_ref[...]
    blocks = blocks_ref[...].astype(F32)
    mask = jnp.concatenate(
        [
            jnp.broadcast_to(blocks[:, b : b + 1], (tokens, FBLK))
            for b in range(columns // FBLK)
        ],
        axis=1,
    )
    value = (mask * total).astype(BF16)
    for part in range(count):
        out_ref[part] = value


def masked_sum(parts, bias, blocks):
    return pl.pallas_call(
        masked_sum_kernel,
        out_shape=jax.ShapeDtypeStruct(parts.shape, BF16),
        name="masked_sum",
    )(parts, bias, blocks)


def weight_specs(near_shape, far_shape, chunk):
    slots, features, cols = near_shape
    far_chunks = far_shape[0] // chunk
    specs = [pl.BlockSpec((slots, chunk, cols), lambda c, *_: (0, c, 0))]
    specs += [pl.BlockSpec((chunk, cols), lambda c, *_: (c, 0))] * (slots - 1)
    specs += [
        pl.BlockSpec((chunk, cols), lambda c, *_: (jnp.minimum(c, far_chunks - 1), 0)),
        pl.BlockSpec((chunk, cols), lambda c, *_: (jnp.maximum(c - far_chunks, 0), 0)),
    ]
    return specs


def decoders_up(step, near_ref, moved_refs, far_ref, far_moved_ref, far_chunks):
    slots = near_ref.shape[0]
    found = [near_ref[0]] + [ref[...] for ref in moved_refs]
    found.append(jnp.where(step < far_chunks, far_ref[...], far_moved_ref[...]))
    found += [near_ref[2 * slots - r] for r in range(slots + 1, 2 * slots)]
    return found


def forward_kernel(far_chunks, place_ref, acts_ref, near_ref, *refs):
    slots = near_ref.shape[0]
    moved_refs, (far_ref, far_moved_ref, out_ref, total_ref) = refs[: slots - 1], refs[slots - 1 :]
    step = pl.program_id(0)
    layers = 2 * slots
    cols = near_ref.shape[2]

    @pl.when(step == 0)
    def _():
        total_ref[...] = jnp.zeros_like(total_ref)

    acts = jnp.concatenate([acts_ref[p] for p in range(acts_ref.shape[0])], axis=1)
    weights = decoders_up(step, near_ref, moved_refs, far_ref, far_moved_ref, far_chunks)
    for pair in range(slots):
        both = jnp.concatenate(weights[2 * pair : 2 * pair + 2], axis=1)
        total_ref[pair] += jnp.dot(acts, both, preferred_element_type=F32)

    @pl.when(step == pl.num_programs(0) - 1)
    def _():
        place = place_ref[0]
        for r in range(layers):
            share = total_ref[r // 2, :, (r % 2) * cols : (r % 2 + 1) * cols]
            kept = jnp.where(place + r < layers, share, 0.0)
            out_ref[lax.rem(place + r, layers)] = kept.astype(BF16)


def forward_shares(place, acts, near, moved, far, far_moved, chunk=512):
    slots, features, cols = near.shape
    parts, tokens, columns = acts.shape
    layers = 2 * slots
    return pl.pallas_call(
        functools.partial(forward_kernel, far.shape[0] // chunk),
        grid=(features // chunk,),
        in_specs=[
            pl.BlockSpec(memory_space=SMEM),
            pl.BlockSpec((chunk // columns, tokens, columns), lambda c: (c, 0, 0)),
            *weight_specs(near.shape, far.shape, chunk),
        ],
        out_specs=pl.BlockSpec((layers, tokens, cols), lambda c: (0, 0, 0)),
        out_shape=jax.ShapeDtypeStruct((layers, tokens, cols), BF16),
        scratch_shapes=[pltpu.VMEM((slots, tokens, 2 * cols), F32)],
        compiler_params=pltpu.CompilerParams(vmem_limit_bytes=VMEM_LIMIT),
        name="forward_shares",
    )(place, acts, near, *moved, far, far_moved)


def residual_kernel(shares_ref, target_ref, rec_ref, grads_ref):
    total = shares_ref[0].astype(F32)
    for part in range(1, shares_ref.shape[0]):
        total = total + shares_ref[part].astype(F32)
    rec_ref[...] = total
    grad = (total - target_ref[...].astype(F32)).astype(BF16)
    for part in range(grads_ref.shape[0]):
        grads_ref[part] = grad


def residual(shares, target):
    return pl.pallas_call(
        residual_kernel,
        out_shape=(
            jax.ShapeDtypeStruct(target.shape, F32),
            jax.ShapeDtypeStruct(shares.shape, BF16),
        ),
        name="residual",
    )(shares, target)


def backward_kernel(far_chunks, place_ref, grads_ref, near_ref, *refs):
    slots = near_ref.shape[0]
    moved_refs, (far_ref, far_moved_ref, out_ref, up_ref) = refs[: slots - 1], refs[slots - 1 :]
    step = pl.program_id(0)
    layers = 2 * slots
    cols = near_ref.shape[2]
    columns = out_ref.shape[2]

    @pl.when(step == 0)
    def _():
        place = place_ref[0]
        for r in range(layers):
            grad = grads_ref[lax.rem(place + r, layers)]
            up_ref[:, r * cols : (r + 1) * cols] = jnp.where(
                place + r < layers, grad, jnp.zeros_like(grad)
            )

    weights = decoders_up(step, near_ref, moved_refs, far_ref, far_moved_ref, far_chunks)
    product = lax.dot_general(
        up_ref[...],
        jnp.concatenate(weights, axis=1),
        (((1,), (1,)), ((), ())),
        preferred_element_type=F32,
    )
    for part in range(out_ref.shape[0]):
        out_ref[part] = product[:, part * columns : (part + 1) * columns].astype(BF16)


def backward_parts(place, grads, near, moved, far, far_moved, parts, chunk=512):
    slots, features, cols = near.shape
    layers, tokens, _ = grads.shape
    columns = features // parts
    return pl.pallas_call(
        functools.partial(backward_kernel, far.shape[0] // chunk),
        grid=(features // chunk,),
        in_specs=[
            pl.BlockSpec(memory_space=SMEM),
            pl.BlockSpec(grads.shape, lambda c: (0, 0, 0)),
            *weight_specs(near.shape, far.shape, chunk),
        ],
        out_specs=pl.BlockSpec((chunk // columns, tokens, columns), lambda c: (c, 0, 0)),
        out_shape=jax.ShapeDtypeStruct((parts, tokens, columns), BF16),
        scratch_shapes=[pltpu.VMEM((tokens, layers * cols), BF16)],
        compiler_params=pltpu.CompilerParams(vmem_limit_bytes=VMEM_LIMIT),
        name="backward_parts",
    )(place, grads, near, *moved, far, far_moved)


def encoder_grad_kernel(in_ref, pre_ref, enc_ref, bias_ref):
    columns = pre_ref.shape[2]
    for part in range(pre_ref.shape[0]):
        grad = pre_ref[part]
        span = slice(part * columns, (part + 1) * columns)
        enc_ref[:, span] = lax.dot_general(
            in_ref[...], grad, (((0,), (0,)), ((), ())), preferred_element_type=F32
        ).astype(BF16)
        bias_ref[:, span] = jnp.sum(grad.astype(F32), axis=0, keepdims=True)


def encoder_grads(local_in, pre_grad):
    tokens, rows = local_in.shape
    parts, _, columns = pre_grad.shape
    step = 4
    return pl.pallas_call(
        encoder_grad_kernel,
        grid=(parts // step,),
        in_specs=[
            pl.BlockSpec((tokens, rows), lambda c: (0, 0)),
            pl.BlockSpec((step, tokens, columns), lambda c: (c, 0, 0)),
        ],
        out_specs=[
            pl.BlockSpec((rows, step * columns), lambda c: (0, c)),
            pl.BlockSpec((1, step * columns), lambda c: (0, c)),
        ],
        out_shape=(
            jax.ShapeDtypeStruct((rows, parts * columns), BF16),
            jax.ShapeDtypeStruct((1, parts * columns), F32),
        ),
        name="encoder_grads",
    )(local_in, pre_grad)


EARLY = (1, 2, 3, 4)


def on_device(inputs, encoder, enc_bias, active_blocks, near_decoders, far_decoders, targets):
    parts = lax.axis_size("width")
    slots = near_decoders.shape[1]
    place = lax.axis_index("blk")[None].astype(jnp.int32)
    column = lax.axis_index("width")
    local_in = inputs[0]
    near, far = near_decoders[0], far_decoders[0]
    columns = encoder.shape[2] // parts
    per_part = columns // FBLK
    blocks = lax.dynamic_slice_in_dim(active_blocks[0], column * per_part, per_part, 1)
    bias = lax.dynamic_slice_in_dim(enc_bias, column * columns, columns, 1)

    moved = {o: shifted_down(near[o], o) for o in range(1, slots)}
    far_moved = shifted_down(far, slots)

    arrived = exchange(pre_parts(local_in, encoder[0], parts), "width")
    act_part = masked_sum(arrived, bias, blocks)
    early = [moved[o] for o in EARLY]
    act_part, early = lax.optimization_barrier((act_part, early))
    moved.update(zip(EARLY, early))
    acts = exchange(act_part, "width")
    moved = [moved[o] for o in range(1, slots)]
    shares = forward_shares(place, acts, near, moved, far, far_moved)
    reconstruction, own_grads = residual(exchange(shares, "blk"), targets[0])
    all_grads = exchange(own_grads, "blk")
    grad_parts = backward_parts(place, all_grads, near, moved, far, far_moved, parts)
    pre_part = masked_sum(exchange(grad_parts, "width"), jnp.zeros_like(bias), blocks)
    enc_grad, bias_grad = encoder_grads(local_in, exchange(pre_part, "width"))
    return reconstruction[None], enc_grad[None], bias_grad


def solution(mesh):
    return jax.shard_map(
        on_device,
        mesh=mesh,
        in_specs=(
            P("blk", None, "width"),
            P("blk", "width", None),
            P("blk", None),
            P("blk", None, None),
            P("blk", None, None, "width"),
            P("blk", None, "width"),
            P("blk", None, "width"),
        ),
        out_specs=(P("blk", None, "width"), P("blk", "width", None), P("blk", None)),
        check_vma=False,
    )
```

time: 417 us -> 335 us (0.80)
  matrix products: 77.3 us -> 0 us
  waiting for transfers between devices: 46.6 us -> 123 us
  starting transfers between devices: 82 us -> 31.2 us
  other arithmetic: 46.2 us -> 0 us
  Pallas kernels: 0 us -> 32.9 us
  local copies, waits for them, and re-layouts: 23.2 us -> 14.4 us
  blocking collectives: 137 us -> 131 us
    ppermute x9 -> x8, waiting for transfers between devices: 0.02 us -> 109 us  [shifted_down(): return lax.ppermute(block, 'blk', route)]
    dot_general x34 -> x0, matrix products: 77.3 us -> none  [the longest x16 47.3 us: backward_product(): lax.dot_general(grads, weights, (((1,), (1,)), ((), ())), preferred_eleme...]
    ppermute x9 -> x8, starting transfers between devices: 62 us -> 10.3 us  [shifted_down(): return lax.ppermute(block, 'blk', route)]
    pallas_call x0 -> x7, Pallas kernels: none -> 32.9 us  [the longest x1 10.1 us: backward_parts(): pl.pallas_call(functools.partial(backward_kernel, far.shape[0] // chunk),...]
    all_to_all x3 -> x2, waiting for transfers between devices: 46.6 us -> 14.4 us  [exchange(): return lax.all_to_all(parts, axis, 0, 0, tiled=True)]
    scatter-add x14 -> x0, other arithmetic: 29.3 us -> none  [the longest x7 14.8 us: on_device(): buffer = buffer.at[(cycle_index + offset) % layers].add(moved_term)]
    convert_element_type x5 -> x0, other arithmetic: 13 us -> none  [the longest x1 9.86 us: on_device(): grad_part = sent_and_summed(own_grad.astype(jnp.bfloat16), 'width', 1)]
    all_to_all x3 -> x4, blocking collectives: 137 us -> 131 us  [exchange(): return lax.all_to_all(parts, axis, 0, 0, tiled=True)]
  transfers between devices with their start and end apart: 12 -> 10, of which waited for: 3 -> 5; matrix products, arithmetic and copies ran while one was open for 29% -> 2% of each run, Pallas kernels for 0% -> 1%
where the time goes in v1:
time: 335 us; the launch traced here: 333 us
  blocking collectives  131 us (39%)
  waiting for transfers between devices  123 us (37%)
  Pallas kernels  32.9 us (10%)
  starting transfers between devices  31.2 us (9%)
  local copies, waits for them, and re-layouts  14.4 us (4%)
    all_to_all x4, blocking collectives, exchange(): return lax.all_to_all(parts, axis, 0, 0, tiled=True)  131 us
    ppermute x8, waiting for transfers between devices, shifted_down(): return lax.ppermute(block, 'blk', route)  109 us
    all_to_all x2, starting transfers between devices, exchange(): return lax.all_to_all(parts, axis, 0, 0, tiled=True)  20.8 us
    all_to_all x2, waiting for transfers between devices, exchange(): return lax.all_to_all(parts, axis, 0, 0, tiled=True)  14.4 us
    ppermute x8, starting transfers between devices, shifted_down(): return lax.ppermute(block, 'blk', route)  10.3 us
    pallas_call x1, Pallas kernels, backward_parts(): pl.pallas_call(functools.partial(backward_kernel, far.shape[0] // chunk),...  10.1 us
    pallas_call x1, Pallas kernels, forward_shares(): pl.pallas_call(functools.partial(forward_kernel, far.shape[0] // chunk),...  8.37 us
  transfers between devices with their start and end apart: 10, of which 5 were waited for; matrix products, arithmetic and copies ran while one was open for 2% of the time, Pallas kernels for 1%

profile of v1, /device:TPU:32, one launch (start us, length us, event | category | flops | bytes accessed | tf_op | source)
XLA Modules:
  0.0 332.9 jit_solution(8748725021593123634)
XLA Ops:
  0.6 3.8 %pre_parts.1 = bf16[16,128,256]{2,1,0:T(8,128)(2,1)} custom-call(bf16[128,128]{1,0:T(8,128)(2,1)} %bitcast.31, bf16[128,4096]{1,0:T(8,128)(2,1)} %bitcast.28), custom_call_target="tpu_custom_call" | custom-call | tf_op jit(solution)/shard_map/pre_parts/pallas_call | solution.py:39
  4.4 11.2 %all-to-all-start = ((bf16[16,128,256]{2,1,0:T(8,128)(2,1)}), bf16[16,128,256]{2,1,0:T(8,128)(2,1)}, u32[]{:S(2)}, u32[]{:S(2)}) async-start(bf16[16,128,256]{2,1,0:T(8,128)(2,1)} %pre_parts.1), calls=%async_computation | async-start | bytes 2097152 | tf_op jit(solution)/shard_map/all_to_all | solution.py:18
  15.6 6.3 %slice_bitcast_fusion = (bf16[4096,128]{1,0:T(8,128)(2,1)}, bf16[4096,128]{1,0:T(8,128)(2,1)}, bf16[4096,128]{1,0:T(8,128)(2,1)}, bf16[4096,128]{1,0:T(8,128)(2,...) fusion(bf16[1,8,4096,128]{3,2,1,0:T(8,128)(2,1)} %param.11), kind=kLoop, calls=%fused_computation | loop fusion | bytes 14680064 | tf_op jit(solution)/shard_map/squeeze | solution.py:263
  21.9 1.3 collective-permute-start
  23.2 1.3 collective-permute-start.1
  24.5 1.3 collective-permute-start.2
  25.8 1.3 collective-permute-start.3
  27.9 1.2 constant_dynamic-slice_fusion.1.bias_ref
  29.1 14.4 %all-to-all-done.parts_ref = bf16[16,128,256]{2,1,0:T(8,128)(2,1)} async-done(((bf16[16,128,256]{2,1,0:T(8,128)(2,1)}), bf16[16,128,256]{2,1,0:T(8,128)(2,1)}, u32[]{:S(2)}, u32[]{:S(2)}) %all-to-all-start) | async-done | bytes 1048608 | tf_op jit(solution)/shard_map/all_to_all | solution.py:18
  43.5 2.4 masked_sum.2
  45.9 24.0 %collective-permute-done.1.refs_1_ = bf16[4096,128]{1,0:T(8,128)(2,1)S(1)} collective-permute-done((bf16[4096,128]{1,0:T(8,128)(2,1)}, bf16[4096,128]{1,0:T(8,128)(2,1)S(1)}, u32[]{:S(2)}, u32[]{:S(2)}) %collective-permute-start.1) | collective-permute-done | bytes 1048608 | tf_op jit(solution)/shard_map/ppermute | solution.py:24
  69.9 2.0 collective-permute-done.2.refs_2_
  73.0 9.6 %all-to-all-start.1 = ((bf16[16,128,256]{2,1,0:T(8,128)(2,1)}), bf16[16,128,256]{2,1,0:T(8,128)(2,1)S(1)}, u32[]{:S(2)}, u32[]{:S(2)}) async-start(bf16[16,128,256]{2,1,0:T(8,128)(2,1)} %masked_sum.2), calls=%async_computation.1 | async-start | bytes 2097152 | tf_op jit(solution)/shard_map/all_to_all | solution.py:18
  82.6 1.3 collective-permute-start.4
  83.9 1.3 collective-permute-start.5
  85.2 1.3 collective-permute-start.6
  86.5 1.3 collective-permute-start.7
  87.8 71.4 %collective-permute-done.7.refs_8_ = bf16[2048,128]{1,0:T(8,128)(2,1)} collective-permute-done((bf16[2048,128]{1,0:T(8,128)(2,1)}, bf16[2048,128]{1,0:T(8,128)(2,1)}, u32[]{:S(2)}, u32[]{:S(2)}) %collective-permute-start.7) | collective-permute-done | bytes 524320 | tf_op jit(solution)/shard_map/ppermute | solution.py:24
  159.2 11.0 %collective-permute-done.5.refs_5_ = bf16[4096,128]{1,0:T(8,128)(2,1)} collective-permute-done((bf16[4096,128]{1,0:T(8,128)(2,1)}, bf16[4096,128]{1,0:T(8,128)(2,1)}, u32[]{:S(2)}, u32[]{:S(2)}) %collective-permute-start.5) | collective-permute-done | bytes 1048608 | tf_op jit(solution)/shard_map/ppermute | solution.py:24
  170.3 1.2 copy-done.2
  171.5 1.0 copy-done.4
  172.5 8.4 %forward_shares.1 = bf16[16,128,128]{2,1,0:T(8,128)(2,1)S(1)} custom-call(s32[1]{0:T(128)} %bitcast.place_ref, bf16[16,128,256]{2,1,0:T(8,128)(2,1)S(1)} %all-to-all-done.1.acts_ref, bf16[8,4096,128]{2,1,0:T(8,128)(2,1)} %bitcast.26, bf16[4096,128]{1,0:T(8,128)(2,1)S(1)} %collective-permute-done.refs_0_, ...), custom_call_target="tpu_custom_call" | custom-call | tf_op jit(solution)/shard_map/forward_shares/pallas_call | solution.py:129
  180.9 47.9 %all_to_all.30.shares_ref = bf16[16,128,128]{2,1,0:T(8,128)(2,1)} all-to-all(bf16[16,128,128]{2,1,0:T(8,128)(2,1)S(1)} %forward_shares.1), channel_id=1, replica_groups=mesh['blk'=16,'width'=16] {'blk'}, dimensions={0} | all-to-all | bytes 1048576 | tf_op jit(solution)/shard_map/all_to_all | solution.py:18
  228.8 2.0 residual.1
  230.8 14.4 %all_to_all.31.grads_ref = bf16[16,128,128]{2,1,0:T(8,128)(2,1)S(1)} all-to-all(bf16[16,128,128]{2,1,0:T(8,128)(2,1)} %get-tuple-element.18), channel_id=1, replica_groups=mesh['blk'=16,'width'=16] {'blk'}, dimensions={0} | all-to-all | bytes 1048576 | tf_op jit(solution)/shard_map/all_to_all | solution.py:18
  245.1 1.2 copy-done.3
  246.4 1.0 copy-done.5
  247.4 10.1 %backward_parts.1 = bf16[16,128,256]{2,1,0:T(8,128)(2,1)S(1)} custom-call(s32[1]{0:T(128)} %bitcast.place_ref, bf16[16,128,128]{2,1,0:T(8,128)(2,1)S(1)} %all_to_all.31.grads_ref, bf16[8,4096,128]{2,1,0:T(8,128)(2,1)} %bitcast.27, bf16[4096,128]{1,0:T(8,128)(2,1)S(1)} %collective-permute-done.refs_0_, bf16[4096,128]{1,0:T(8,128)(2,1)S(1)} %collective-permute-done.1.refs_1_, ...), custom_call_target="tpu_custom_call" | custom-call | tf_op jit(solution)/shard_map/backward_parts/pallas_call | solution.py:198
  257.5 36.9 %all_to_all.32.parts_ref = bf16[16,128,256]{2,1,0:T(8,128)(2,1)} all-to-all(bf16[16,128,256]{2,1,0:T(8,128)(2,1)S(1)} %backward_parts.1), channel_id=1, replica_groups=mesh['blk'=16,'width'=16] {'width'}, dimensions={0} | all-to-all | bytes 2097152 | tf_op jit(solution)/shard_map/all_to_all | solution.py:18
  295.0 2.4 masked_sum.3
  297.4 31.7 %all_to_all.33.pre_ref = bf16[16,128,256]{2,1,0:T(8,128)(2,1)} all-to-all(bf16[16,128,256]{2,1,0:T(8,128)(2,1)} %masked_sum.3), channel_id=1, replica_groups=mesh['blk'=16,'width'=16] {'width'}, dimensions={0} | all-to-all | bytes 2097152 | tf_op jit(solution)/shard_map/all_to_all | solution.py:18
  329.1 3.8 %encoder_grads.1 = (bf16[128,4096]{1,0:T(8,128)(2,1)}, f32[1,4096]{1,0:T(1,128)}) custom-call(bf16[128,128]{1,0:T(8,128)(2,1)} %bitcast.32, bf16[16,128,256]{2,1,0:T(8,128)(2,1)} %all_to_all.33.pre_ref), custom_call_target="tpu_custom_call" | custom-call | tf_op jit(solution)/shard_map/encoder_grads/pallas_call | solution.py:229
  (16 shorter events, 2.3 us)
Async XLA Ops:
  0.6 26.5 %copy-start = (s32[1,128,32]{1,2,0:T(8,128)S(1)}, s32[1,128,32]{1,2,0:T(8,128)}, u32[]{:S(2)}) copy-start(s32[1,128,32]{1,2,0:T(8,128)} %param.10) | copy-start | bytes 49156
  4.4 39.1 %all-to-all-start = ((bf16[16,128,256]{2,1,0:T(8,128)(2,1)}), bf16[16,128,256]{2,1,0:T(8,128)(2,1)}, u32[]{:S(2)}, u32[]{:S(2)}) async-start(bf16[16,128,256]{2,1,0:T(8,128)(2,1)} %pre_parts.1), calls=%async_computation | async-start | bytes 2097152 | tf_op jit(solution)/shard_map/all_to_all | solution.py:18
  21.9 24.0 %collective-permute-start = (bf16[4096,128]{1,0:T(8,128)(2,1)}, bf16[4096,128]{1,0:T(8,128)(2,1)S(1)}, u32[]{:S(2)}, u32[]{:S(2)}) collective-permute-start(bf16[4096,128]{1,0:T(8,128)(2,1)} %get-tuple-element.26), channel_id=1, source_target_pairs={{16,0},{32,16},{48,32},{64,48},{80,64},{96,80},{112,96},{128,112},... | collective-permute-start | bytes 3145736 | tf_op jit(solution)/shard_map/ppermute | solution.py:24
  23.2 46.7 %collective-permute-start.1 = (bf16[4096,128]{1,0:T(8,128)(2,1)}, bf16[4096,128]{1,0:T(8,128)(2,1)S(1)}, u32[]{:S(2)}, u32[]{:S(2)}) collective-permute-start(bf16[4096,128]{1,0:T(8,128)(2,1)} %get-tuple-element.25), channel_id=1, source_target_pairs={{32,0},{48,16},{64,32},{80,48},{96,64},{112,80},{128,96},{144,112}... | collective-permute-start | bytes 3145736 | tf_op jit(solution)/shard_map/ppermute | solution.py:24
  24.5 47.5 %collective-permute-start.2 = (bf16[4096,128]{1,0:T(8,128)(2,1)}, bf16[4096,128]{1,0:T(8,128)(2,1)S(1)}, u32[]{:S(2)}, u32[]{:S(2)}) collective-permute-start(bf16[4096,128]{1,0:T(8,128)(2,1)} %get-tuple-element.24), channel_id=1, source_target_pairs={{48,0},{64,16},{80,32},{96,48},{112,64},{128,80},{144,96},{160,112... | collective-permute-start | bytes 3145736 | tf_op jit(solution)/shard_map/ppermute | solution.py:24
  25.8 47.2 %collective-permute-start.3 = (bf16[4096,128]{1,0:T(8,128)(2,1)}, bf16[4096,128]{1,0:T(8,128)(2,1)}, u32[]{:S(2)}, u32[]{:S(2)}) collective-permute-start(bf16[4096,128]{1,0:T(8,128)(2,1)} %get-tuple-element.23), channel_id=1, source_target_pairs={{64,0},{80,16},{96,32},{112,48},{128,64},{144,80},{160,96},{176,11... | collective-permute-start | bytes 3145736 | tf_op jit(solution)/shard_map/ppermute | solution.py:24
  72.0 1.0 copy-start.1
  73.0 97.3 %all-to-all-start.1 = ((bf16[16,128,256]{2,1,0:T(8,128)(2,1)}), bf16[16,128,256]{2,1,0:T(8,128)(2,1)S(1)}, u32[]{:S(2)}, u32[]{:S(2)}) async-start(bf16[16,128,256]{2,1,0:T(8,128)(2,1)} %masked_sum.2), calls=%async_computation.1 | async-start | bytes 2097152 | tf_op jit(solution)/shard_map/all_to_all | solution.py:18
  82.6 76.6 %collective-permute-start.4 = (bf16[4096,128]{1,0:T(8,128)(2,1)}, bf16[4096,128]{1,0:T(8,128)(2,1)}, u32[]{:S(2)}, u32[]{:S(2)}) collective-permute-start(bf16[4096,128]{1,0:T(8,128)(2,1)} %get-tuple-element.22), channel_id=1, source_target_pairs={{80,0},{96,16},{112,32},{128,48},{144,64},{160,80},{176,96},{192,1... | collective-permute-start | bytes 3145736 | tf_op jit(solution)/shard_map/ppermute | solution.py:24
  83.9 86.3 %collective-permute-start.5 = (bf16[4096,128]{1,0:T(8,128)(2,1)}, bf16[4096,128]{1,0:T(8,128)(2,1)}, u32[]{:S(2)}, u32[]{:S(2)}) collective-permute-start(bf16[4096,128]{1,0:T(8,128)(2,1)} %get-tuple-element.27), channel_id=1, source_target_pairs={{96,0},{112,16},{128,32},{144,48},{160,64},{176,80},{192,96},{208,... | collective-permute-start | bytes 3145736 | tf_op jit(solution)/shard_map/ppermute | solution.py:24
  85.2 85.0 %collective-permute-start.6 = (bf16[4096,128]{1,0:T(8,128)(2,1)}, bf16[4096,128]{1,0:T(8,128)(2,1)}, u32[]{:S(2)}, u32[]{:S(2)}) collective-permute-start(bf16[4096,128]{1,0:T(8,128)(2,1)} %get-tuple-element.21), channel_id=1, source_target_pairs={{112,0},{128,16},{144,32},{160,48},{176,64},{192,80},{208,96},{224... | collective-permute-start | bytes 3145736 | tf_op jit(solution)/shard_map/ppermute | solution.py:24
  86.5 72.7 %collective-permute-start.7 = (bf16[2048,128]{1,0:T(8,128)(2,1)}, bf16[2048,128]{1,0:T(8,128)(2,1)}, u32[]{:S(2)}, u32[]{:S(2)}) collective-permute-start(bf16[2048,128]{1,0:T(8,128)(2,1)} %bitcast.23), channel_id=1, source_target_pairs={{128,0},{144,16},{160,32},{176,48},{192,64},{208,80},{224,96},{240... | collective-permute-start | bytes 1572872 | tf_op jit(solution)/shard_map/ppermute | solution.py:24
  170.3 1.2 copy-start.2
  171.5 1.0 copy-start.4
  245.1 1.2 copy-start.3
  246.4 1.0 copy-start.5

commit v2 on v1

--- a/solution.py
+++ b/solution.py
@@ -10,18 +10,37 @@
 FBLK = 128
 BF16 = jnp.bfloat16
 F32 = jnp.float32
+HALVES = 2
 SMEM = pltpu.MemorySpace.SMEM
 VMEM_LIMIT = 40 * 1024 * 1024
 
 
-def exchange(parts, axis):
-    return lax.all_to_all(parts, axis, 0, 0, tiled=True)
-
-
-def shifted_down(block, distance, lowest=0):
-    count = lax.axis_size("blk")
-    route = [(i, i - distance) for i in range(count) if i - distance >= lowest]
-    return lax.ppermute(block, "blk", route)
+def exchange(parts, axis, runs=1):
+    count = lax.axis_size(axis) // runs
+    groups = [list(range(r * count, (r + 1) * count)) for r in range(runs)]
+    return lax.all_to_all(parts, axis, 0, 0, tiled=True, axis_index_groups=groups)
+
+
+def crossed(low, high, layers):
+    spread = high - low
+    half = layers // 2
+    return (low < half) & (high >= half) & (low % 2 == 1) & (spread < half)
+
+
+def shifted_down(block, distance):
+    layers, parts = lax.axis_size("blk"), lax.axis_size("width")
+    route = []
+    for high in range(distance, layers):
+        low = high - distance
+        turn = parts // 2 if crossed(low, high, layers) else 0
+        for part in range(parts):
+            route.append((high * parts + part, low * parts + (part + turn) % parts))
+    return lax.ppermute(block, ("blk", "width"), route)
+
+
+def other_half(block):
+    parts = lax.axis_size("width")
+    return lax.ppermute(block, "width", [(p, (p + parts // 2) % parts) for p in range(parts)])
 
 
 def pre_kernel(in_ref, enc_ref, out_ref):
@@ -35,7 +54,7 @@
     tokens, rows = local_in.shape
     features = encoder.shape[1]
     columns = features // parts
-    step = 4
+    step = 2
     return pl.pallas_call(
         pre_kernel,
         grid=(parts // step,),
@@ -49,12 +68,24 @@
     )(local_in, encoder)
 
 
-def masked_sum_kernel(parts_ref, bias_ref, blocks_ref, out_ref):
-    count, tokens, columns = parts_ref.shape
+def part_sum_kernel(parts_ref, out_ref):
     total = parts_ref[0].astype(F32)
-    for part in range(1, count):
+    for part in range(1, parts_ref.shape[0]):
         total = total + parts_ref[part].astype(F32)
-    total = total + bias_ref[...]
+    out_ref[...] = total.astype(BF16)
+
+
+def part_sum(parts):
+    return pl.pallas_call(
+        part_sum_kernel,
+        out_shape=jax.ShapeDtypeStruct(parts.shape[1:], BF16),
+        name="part_sum",
+    )(parts)
+
+
+def masked_sum_kernel(own_ref, came_ref, bias_ref, blocks_ref, out_ref):
+    tokens, columns = own_ref.shape
+    total = own_ref[...].astype(F32) + came_ref[...].astype(F32) + bias_ref[...]
     blocks = blocks_ref[...].astype(F32)
     mask = jnp.concatenate(
         [
@@ -64,16 +95,21 @@
         axis=1,
     )
     value = (mask * total).astype(BF16)
-    for part in range(count):
+    for part in range(out_ref.shape[0]):
         out_ref[part] = value
 
 
-def masked_sum(parts, bias, blocks):
+def masked_sum(own, came, bias, blocks, parts):
     return pl.pallas_call(
         masked_sum_kernel,
-        out_shape=jax.ShapeDtypeStruct(parts.shape, BF16),
+        out_shape=jax.ShapeDtypeStruct((parts, *own.shape), BF16),
         name="masked_sum",
-    )(parts, bias, blocks)
+    )(own, came, bias, blocks)
+
+
+def summed_over_width(parts, bias, blocks):
+    own = part_sum(exchange(parts, "width", HALVES))
+    return exchange(masked_sum(own, other_half(own), bias, blocks, parts.shape[0]), "width", HALVES)
 
 
 def weight_specs(near_shape, far_shape, chunk):
@@ -142,25 +178,60 @@
     )(place, acts, near, *moved, far, far_moved)
 
 
-def residual_kernel(shares_ref, target_ref, rec_ref, grads_ref):
-    total = shares_ref[0].astype(F32)
-    for part in range(1, shares_ref.shape[0]):
-        total = total + shares_ref[part].astype(F32)
-    rec_ref[...] = total
-    grad = (total - target_ref[...].astype(F32)).astype(BF16)
-    for part in range(grads_ref.shape[0]):
-        grads_ref[part] = grad
-
-
-def residual(shares, target):
+def share_sums_kernel(place_ref, shares_ref, own_ref, other_ref, sent_ref):
+    layers = shares_ref.shape[0]
+    place = place_ref[0]
+    own = jnp.zeros(own_ref.shape, F32)
+    other = jnp.zeros(own_ref.shape, F32)
+    for low in range(layers):
+        share = shares_ref[low].astype(F32)
+        away = crossed(low, place, layers)
+        own = own + jnp.where(away, 0.0, share)
+        other = other + jnp.where(away, share, 0.0)
+    own_ref[...] = own
+    other_ref[...] = other
+    sent_ref[0] = own.astype(BF16)
+    sent_ref[1] = other.astype(BF16)
+
+
+def share_sums(place, shares):
+    _, tokens, cols = shares.shape
+    return pl.pallas_call(
+        share_sums_kernel,
+        in_specs=[pl.BlockSpec(memory_space=SMEM), pl.BlockSpec(memory_space=pltpu.VMEM)],
+        out_shape=(
+            jax.ShapeDtypeStruct((tokens, cols), F32),
+            jax.ShapeDtypeStruct((tokens, cols), F32),
+            jax.ShapeDtypeStruct((2, tokens, cols), BF16),
+        ),
+        name="share_sums",
+    )(place, shares)
+
+
+def residual_kernel(place_ref, own_ref, other_ref, came_ref, target_ref, away_target_ref, rec_ref, grads_ref):
+    layers = grads_ref.shape[0]
+    place = place_ref[0]
+    rec = own_ref[...] + came_ref[1].astype(F32)
+    away_rec = other_ref[...] + came_ref[0].astype(F32)
+    rec_ref[...] = rec
+    grad = (rec - target_ref[...].astype(F32)).astype(BF16)
+    away_grad = (away_rec - away_target_ref[...].astype(F32)).astype(BF16)
+    for low in range(layers):
+        grads_ref[low] = jnp.where(crossed(low, place, layers), away_grad, grad)
+
+
+def residual(place, own, other, came, target, away_target):
+    layers = lax.axis_size("blk")
+    vmem = pl.BlockSpec(memory_space=pltpu.VMEM)
     return pl.pallas_call(
         residual_kernel,
+        in_specs=[pl.BlockSpec(memory_space=SMEM)] + [vmem] * 5,
         out_shape=(
             jax.ShapeDtypeStruct(target.shape, F32),
-            jax.ShapeDtypeStruct(shares.shape, BF16),
+            jax.ShapeDtypeStruct((layers, *target.shape), BF16),
         ),
         name="residual",
-    )(shares, target)
+    )(place, own, other, came, target, away_target)
 
 
 def backward_kernel(far_chunks, place_ref, grads_ref, near_ref, *refs):
@@ -225,7 +296,7 @@
 def encoder_grads(local_in, pre_grad):
     tokens, rows = local_in.shape
     parts, _, columns = pre_grad.shape
-    step = 4
+    step = 2
     return pl.pallas_call(
         encoder_grad_kernel,
         grid=(parts // step,),
@@ -245,14 +316,15 @@
     )(local_in, pre_grad)
 
 
-EARLY = (1, 2, 3, 4)
+FIRST = (1, 7)
+LANES = ((2, 3), (6, 5), (4, 8))
 
 
 def on_device(inputs, encoder, enc_bias, active_blocks, near_decoders, far_decoders, targets):
-    parts = lax.axis_size("width")
+    parts = lax.axis_size("width") // HALVES
     slots = near_decoders.shape[1]
     place = lax.axis_index("blk")[None].astype(jnp.int32)
-    column = lax.axis_index("width")
+    column = lax.axis_index("width") % parts
     local_in = inputs[0]
     near, far = near_decoders[0], far_decoders[0]
     columns = encoder.shape[2] // parts
@@ -260,22 +332,33 @@
     blocks = lax.dynamic_slice_in_dim(active_blocks[0], column * per_part, per_part, 1)
     bias = lax.dynamic_slice_in_dim(enc_bias, column * columns, columns, 1)
 
-    moved = {o: shifted_down(near[o], o) for o in range(1, slots)}
-    far_moved = shifted_down(far, slots)
-
-    arrived = exchange(pre_parts(local_in, encoder[0], parts), "width")
-    act_part = masked_sum(arrived, bias, blocks)
-    early = [moved[o] for o in EARLY]
-    act_part, early = lax.optimization_barrier((act_part, early))
-    moved.update(zip(EARLY, early))
-    acts = exchange(act_part, "width")
+    first = [near[o] for o in FIRST]
+    first, rest, local_in = lax.optimization_barrier((first, near, local_in))
+    moved = {o: shifted_down(slot, o) for o, slot in zip(FIRST, first)}
+    parted = pre_parts(local_in, encoder[0], parts)
+    parted, early = lax.optimization_barrier((parted, [moved[o] for o in FIRST]))
+    moved.update(zip(FIRST, early))
+    for lane in LANES:
+        before = None
+        for o in lane:
+            slot = far if o == slots else rest[o]
+            if before:
+                slot, moved[before] = lax.optimization_barrier((slot, moved[before]))
+            moved[o] = shifted_down(slot, o)
+            before = o
+    far_moved = moved[slots]
+
+    acts = summed_over_width(parted, bias, blocks)
     moved = [moved[o] for o in range(1, slots)]
     shares = forward_shares(place, acts, near, moved, far, far_moved)
-    reconstruction, own_grads = residual(exchange(shares, "blk"), targets[0])
+    own, other, sent = share_sums(place, exchange(shares, "blk"))
+    reconstruction, own_grads = residual(
+        place, own, other, other_half(sent), targets[0], other_half(targets[0])
+    )
     all_grads = exchange(own_grads, "blk")
     grad_parts = backward_parts(place, all_grads, near, moved, far, far_moved, parts)
-    pre_part = masked_sum(exchange(grad_parts, "width"), jnp.zeros_like(bias), blocks)
-    enc_grad, bias_grad = encoder_grads(local_in, exchange(pre_part, "width"))
+    pre_grad = summed_over_width(grad_parts, jnp.zeros_like(bias), blocks)
+    enc_grad, bias_grad = encoder_grads(local_in, pre_grad)
     return reconstruction[None], enc_grad[None], bias_grad
 
 

time: 335 us -> 292 us (0.87)
  waiting for transfers between devices: 123 us -> 84.3 us
  blocking collectives: 131 us -> 112 us
  Pallas kernels: 32.9 us -> 38 us
  local copies, waits for them, and re-layouts: 14.4 us -> 17.9 us
    ppermute x8 -> x12, waiting for transfers between devices: 109 us -> 63.9 us  [the longest x8 54.9 us: shifted_down(): return lax.ppermute(block, ('blk', 'width'), route)]
    all_to_all x4, blocking collectives: 131 us -> 112 us  [exchange(): lax.all_to_all(parts, axis, 0, 0, tiled=True, axis_index_groups=groups)]
    ppermute x8 -> x12, starting transfers between devices: 10.3 us -> 20.1 us  [the longest x8 10.3 us: shifted_down(): return lax.ppermute(block, ('blk', 'width'), route)]
    all_to_all x2, starting transfers between devices: 20.8 us -> 13.7 us  [exchange(): lax.all_to_all(parts, axis, 0, 0, tiled=True, axis_index_groups=groups)]
    all_to_all x2, waiting for transfers between devices: 14.4 us -> 20.4 us  [exchange(): lax.all_to_all(parts, axis, 0, 0, tiled=True, axis_index_groups=groups)]
    pallas_call x3 -> x6, Pallas kernels: 6.77 us -> 11.9 us  [the longest x2 4.28 us: masked_sum(): pl.pallas_call(masked_sum_kernel, out_shape=jax.ShapeDtypeStruct((parts,...]
    unnamed x12 -> x24, local copies, waits for them, and re-layouts: 5.55 us -> 7.83 us
    squeeze x1 -> x2, local copies, waits for them, and re-layouts: 6.28 us -> 7.5 us  [the longest x1 4.84 us: on_device(): slot = far if o == slots else rest[o]]
  transfers between devices with their start and end apart: 10 -> 14, of which waited for: 5 -> 8; matrix products, arithmetic and copies ran while one was open for 2% -> 2% of each run, Pallas kernels for 1% -> 3%
where the time goes in v2:
time: 292 us; the launch traced here: 287 us
  blocking collectives  112 us (38%)
  waiting for transfers between devices  84.3 us (29%)
  Pallas kernels  38 us (13%)
  starting transfers between devices  33.8 us (12%)
  local copies, waits for them, and re-layouts  17.9 us (6%)
    all_to_all x4, blocking collectives, exchange(): lax.all_to_all(parts, axis, 0, 0, tiled=True, axis_index_groups=groups)  112 us
    ppermute x8, waiting for transfers between devices, shifted_down(): return lax.ppermute(block, ('blk', 'width'), route)  54.9 us
    all_to_all x2, waiting for transfers between devices, exchange(): lax.all_to_all(parts, axis, 0, 0, tiled=True, axis_index_groups=groups)  20.4 us
    all_to_all x2, starting transfers between devices, exchange(): lax.all_to_all(parts, axis, 0, 0, tiled=True, axis_index_groups=groups)  13.7 us
    ppermute x8, starting transfers between devices, shifted_down(): return lax.ppermute(block, ('blk', 'width'), route)  10.3 us
    pallas_call x1, Pallas kernels, backward_parts(): pl.pallas_call(functools.partial(backward_kernel, far.shape[0] // chunk),...  10.1 us
    ppermute x4, starting transfers between devices, other_half(): lax.ppermute(block, 'width', [(p, (p + parts // 2) % parts) for p in rang...  9.84 us
    ppermute x4, waiting for transfers between devices, other_half(): lax.ppermute(block, 'width', [(p, (p + parts // 2) % parts) for p in rang...  8.94 us
  transfers between devices with their start and end apart: 14, of which 8 were waited for; matrix products, arithmetic and copies ran while one was open for 2% of the time, Pallas kernels for 3%

profile of v2, /device:TPU:32, one launch (start us, length us, event | category | flops | bytes accessed | tf_op | source)
XLA Modules:
  0.0 287.1 jit_solution(9008829278080763281)
XLA Ops:
  0.6 2.7 slice_bitcast_fusion.5
  4.6 1.3 collective-permute-start.1
  5.9 3.8 %pre_parts.1 = bf16[8,128,512]{2,1,0:T(8,128)(2,1)} custom-call(bf16[128,128]{1,0:T(8,128)(2,1)} %bitcast.32, bf16[128,4096]{1,0:T(8,128)(2,1)} %bitcast.29), custom_call_target="tpu_custom_call" | custom-call | tf_op jit(solution)/shard_map/pre_parts/pallas_call | solution.py:58
  9.7 12.8 %collective-permute-done.1.refs_6_ = bf16[4096,128]{1,0:T(8,128)(2,1)S(1)} collective-permute-done((bf16[4096,128]{1,0:T(8,128)(2,1)S(1)}, bf16[4096,128]{1,0:T(8,128)(2,1)S(1)}, u32[]{:S(2)}, u32[]{:S(2)}) %collective-permute-start.1) | collective-permute-done | bytes 1048608 | tf_op jit(solution)/shard_map/ppermute | solution.py:38
  22.5 8.6 %all-to-all-start = ((bf16[8,128,512]{2,1,0:T(8,128)(2,1)}), bf16[8,128,512]{2,1,0:T(8,128)(2,1)S(1)}, u32[]{:S(2)}, u32[]{:S(2)}) async-start(bf16[8,128,512]{2,1,0:T(8,128)(2,1)} %pre_parts.1), calls=%async_computation | async-start | bytes 2097152 | tf_op jit(solution)/shard_map/all_to_all | solution.py:21
  31.0 4.8 %slice_bitcast_fusion = (bf16[4096,128]{1,0:T(8,128)(2,1)}, bf16[4096,128]{1,0:T(8,128)(2,1)}, bf16[4096,128]{1,0:T(8,128)(2,1)}, bf16[4096,128]{1,0:T(8,128)(2,1)}, bf16[4096,128]{1,0:T(8,128)(2,1)}) fusion(bf16[8,4096,128]{2,1,0:T(8,128)(2,1)} %bitcast.26), kind=kLoop, calls=%fused_computation | loop fusion | bytes 10485760 | tf_op jit(solution)/shard_map/squeeze | solution.py:344
  37.2 1.3 collective-permute-start.6
  38.5 20.4 %all-to-all-done.parts_ref = bf16[8,128,512]{2,1,0:T(8,128)(2,1)S(1)} async-done(((bf16[8,128,512]{2,1,0:T(8,128)(2,1)}), bf16[8,128,512]{2,1,0:T(8,128)(2,1)S(1)}, u32[]{:S(2)}, u32[]{:S(2)}) %all-to-all-start) | async-done | bytes 1048608 | tf_op jit(solution)/shard_map/all_to_all | solution.py:21
  59.9 2.0 part_sum.2.own_ref
  61.9 3.7 %collective-permute-start.2 = (bf16[128,512]{1,0:T(8,128)(2,1)}, bf16[128,512]{1,0:T(8,128)(2,1)S(1)}, u32[]{:S(2)}, u32[]{:S(2)}) collective-permute-start(bf16[128,512]{1,0:T(8,128)(2,1)} %part_sum.2.own_ref), channel_id=1, source_target_pairs={{0,8},{1,9},{2,10},{3,11},{4,12},{5,13},{6,14},{7,15},{8,0},{9,1},... | collective-permute-start | bytes 393224 | tf_op jit(solution)/shard_map/ppermute | solution.py:43
  67.6 2.1 collective-permute-done.2.came_ref
  70.3 2.1 masked_sum.2
  72.4 5.1 %all-to-all-start.1 = ((bf16[8,128,512]{2,1,0:T(8,128)(2,1)}), bf16[8,128,512]{2,1,0:T(8,128)(2,1)S(1)}, u32[]{:S(2)}, u32[]{:S(2)}) async-start(bf16[8,128,512]{2,1,0:T(8,128)(2,1)} %masked_sum.2), calls=%async_computation.1 | async-start | bytes 2097152 | tf_op jit(solution)/shard_map/all_to_all | solution.py:21
  78.9 1.3 collective-permute-start.4
  81.5 25.9 %collective-permute-done.5.refs_3_ = bf16[4096,128]{1,0:T(8,128)(2,1)S(1)} collective-permute-done((bf16[4096,128]{1,0:T(8,128)(2,1)}, bf16[4096,128]{1,0:T(8,128)(2,1)S(1)}, u32[]{:S(2)}, u32[]{:S(2)}) %collective-permute-start.5) | collective-permute-done | bytes 1048608 | tf_op jit(solution)/shard_map/ppermute | solution.py:38
  109.6 10.7 %collective-permute-done.8.refs_8_ = bf16[2048,128]{1,0:T(8,128)(2,1)} collective-permute-done((bf16[2048,128]{1,0:T(8,128)(2,1)}, bf16[2048,128]{1,0:T(8,128)(2,1)}, u32[]{:S(2)}, u32[]{:S(2)}) %collective-permute-start.8) | collective-permute-done | bytes 524320 | tf_op jit(solution)/shard_map/ppermute | solution.py:38
  120.4 5.5 %collective-permute-done.7.refs_4_ = bf16[4096,128]{1,0:T(8,128)(2,1)} collective-permute-done((bf16[4096,128]{1,0:T(8,128)(2,1)}, bf16[4096,128]{1,0:T(8,128)(2,1)}, u32[]{:S(2)}, u32[]{:S(2)}) %collective-permute-start.7) | collective-permute-done | bytes 1048608 | tf_op jit(solution)/shard_map/ppermute | solution.py:38
  128.2 8.4 %forward_shares.1 = bf16[16,128,128]{2,1,0:T(8,128)(2,1)S(1)} custom-call(s32[1]{0:T(128)} %bitcast.place_ref, bf16[8,128,512]{2,1,0:T(8,128)(2,1)S(1)} %all-to-all-done.1.acts_ref, bf16[8,4096,128]{2,1,0:T(8,128)(2,1)} %bitcast.27, bf16[4096,128]{1,0:T(8,128)(2,1)S(1)} %collective-permute-done.refs_0_, bf16[4096,128]{1,0:T(8,128)(2,1)} %collective-permute-done.3.refs_1_, ...), custom_call_target="tpu_custom_call" | custom-call | tf_op jit(solution)/shard_map/forward_shares/pallas_call | solution.py:165
  136.5 34.1 %all_to_all.30.shares_ref = bf16[16,128,128]{2,1,0:T(8,128)(2,1)} all-to-all(bf16[16,128,128]{2,1,0:T(8,128)(2,1)S(1)} %forward_shares.1), channel_id=1, replica_groups={{0,16,32,48,64,80,96,112,128,144,160,176,192,208,224,240},{1,17,33,49,6..., dimensions={0} | all-to-all | bytes 1048576 | tf_op jit(solution)/shard_map/all_to_all | solution.py:21
  170.6 1.8 share_sums.1
  173.2 2.7 collective-permute-start.10
  175.9 2.8 collective-permute-done.10.away_target_ref
  179.4 1.8 residual.1
  181.2 14.4 %all_to_all.31.grads_ref = bf16[16,128,128]{2,1,0:T(8,128)(2,1)S(1)} all-to-all(bf16[16,128,128]{2,1,0:T(8,128)(2,1)} %get-tuple-element.40), channel_id=1, replica_groups={{0,16,32,48,64,80,96,112,128,144,160,176,192,208,224,240},{1,17,33,49,6..., dimensions={0} | all-to-all | bytes 1048576 | tf_op jit(solution)/shard_map/all_to_all | solution.py:21
  197.8 10.1 %backward_parts.1 = bf16[8,128,512]{2,1,0:T(8,128)(2,1)S(1)} custom-call(s32[1]{0:T(128)} %bitcast.place_ref, bf16[16,128,128]{2,1,0:T(8,128)(2,1)S(1)} %all_to_all.31.grads_ref, bf16[8,4096,128]{2,1,0:T(8,128)(2,1)} %bitcast.28, bf16[4096,128]{1,0:T(8,128)(2,1)S(1)} %collective-permute-done.refs_0_, bf16[4096,128]{1,0:T(8,128)(2,1)} %collective-permute-done.3.refs_1_, ...), custom_call_target="tpu_custom_call" | custom-call | tf_op jit(solution)/shard_map/backward_parts/pallas_call | solution.py:269
  207.9 34.0 %all_to_all.32.parts_ref = bf16[8,128,512]{2,1,0:T(8,128)(2,1)} all-to-all(bf16[8,128,512]{2,1,0:T(8,128)(2,1)S(1)} %backward_parts.1), channel_id=1, replica_groups={{0,1,2,3,4,5,6,7},{8,9,10,11,12,13,14,15},{16,17,18,19,20,21,22,23},{24..., dimensions={0} | all-to-all | bytes 2097152 | tf_op jit(solution)/shard_map/all_to_all | solution.py:21
  242.0 2.0 part_sum.3.own_ref
  244.0 2.6 collective-permute-start.11
  246.6 4.1 %collective-permute-done.11.came_ref = bf16[128,512]{1,0:T(8,128)(2,1)S(1)} collective-permute-done((bf16[128,512]{1,0:T(8,128)(2,1)}, bf16[128,512]{1,0:T(8,128)(2,1)S(1)}, u32[]{:S(2)}, u32[]{:S(2)}) %collective-permute-start.11) | collective-permute-done | bytes 131104 | tf_op jit(solution)/shard_map/ppermute | solution.py:43
  251.3 2.1 masked_sum.3
  253.4 29.8 %all_to_all.33.pre_ref = bf16[8,128,512]{2,1,0:T(8,128)(2,1)} all-to-all(bf16[8,128,512]{2,1,0:T(8,128)(2,1)} %masked_sum.3), channel_id=1, replica_groups={{0,1,2,3,4,5,6,7},{8,9,10,11,12,13,14,15},{16,17,18,19,20,21,22,23},{24..., dimensions={0} | all-to-all | bytes 2097152 | tf_op jit(solution)/shard_map/all_to_all | solution.py:21
  283.2 3.8 %encoder_grads.1 = (bf16[128,4096]{1,0:T(8,128)(2,1)}, f32[1,4096]{1,0:T(1,128)}) custom-call(bf16[128,128]{1,0:T(8,128)(2,1)} %bitcast.33, bf16[8,128,512]{2,1,0:T(8,128)(2,1)} %all_to_all.33.pre_ref), custom_call_target="tpu_custom_call" | custom-call | tf_op jit(solution)/shard_map/encoder_grads/pallas_call | solution.py:300
  (40 shorter events, 17.7 us)
Async XLA Ops:
  0.6 64.9 %copy-start = (s32[1,128,32]{1,2,0:T(8,128)S(1)}, s32[1,128,32]{1,2,0:T(8,128)}, u32[]{:S(2)}) copy-start(s32[1,128,32]{1,2,0:T(8,128)} %param.10) | copy-start | bytes 49156
  3.3 6.4 %collective-permute-start = (bf16[4096,128]{1,0:T(8,128)(2,1)}, bf16[4096,128]{1,0:T(8,128)(2,1)S(1)}, u32[]{:S(2)}, u32[]{:S(2)}) collective-permute-start(bf16[4096,128]{1,0:T(8,128)(2,1)} %get-tuple-element.24), channel_id=1, source_target_pairs={{16,0},{17,1},{18,2},{19,3},{20,4},{21,5},{22,6},{23,7},{24,8},{25... | collective-permute-start | bytes 3145736 | tf_op jit(solution)/shard_map/ppermute | solution.py:38
  4.6 17.9 %collective-permute-start.1 = (bf16[4096,128]{1,0:T(8,128)(2,1)S(1)}, bf16[4096,128]{1,0:T(8,128)(2,1)S(1)}, u32[]{:S(2)}, u32[]{:S(2)}) collective-permute-start(bf16[4096,128]{1,0:T(8,128)(2,1)S(1)} %get-tuple-element.25), channel_id=1, source_target_pairs={{112,0},{113,1},{114,2},{115,3},{116,4},{117,5},{118,6},{119,7},{1... | collective-permute-start | bytes 3145736 | tf_op jit(solution)/shard_map/ppermute | solution.py:38
  22.5 36.4 %all-to-all-start = ((bf16[8,128,512]{2,1,0:T(8,128)(2,1)}), bf16[8,128,512]{2,1,0:T(8,128)(2,1)S(1)}, u32[]{:S(2)}, u32[]{:S(2)}) async-start(bf16[8,128,512]{2,1,0:T(8,128)(2,1)} %pre_parts.1), calls=%async_computation | async-start | bytes 2097152 | tf_op jit(solution)/shard_map/all_to_all | solution.py:21
  35.9 43.0 %collective-permute-start.3 = (bf16[4096,128]{1,0:T(8,128)(2,1)}, bf16[4096,128]{1,0:T(8,128)(2,1)}, u32[]{:S(2)}, u32[]{:S(2)}) collective-permute-start(bf16[4096,128]{1,0:T(8,128)(2,1)} %get-tuple-element.46), channel_id=1, source_target_pairs={{32,0},{33,1},{34,2},{35,3},{36,4},{37,5},{38,6},{39,7},{40,8},{41... | collective-permute-start | bytes 3145736 | tf_op jit(solution)/shard_map/ppermute | solution.py:38
  37.2 43.0 %collective-permute-start.6 = (bf16[4096,128]{1,0:T(8,128)(2,1)}, bf16[4096,128]{1,0:T(8,128)(2,1)}, u32[]{:S(2)}, u32[]{:S(2)}) collective-permute-start(bf16[4096,128]{1,0:T(8,128)(2,1)} %get-tuple-element.43), channel_id=1, source_target_pairs={{96,0},{97,1},{98,2},{99,3},{100,4},{101,5},{102,6},{103,7},{104,8... | collective-permute-start | bytes 3145736 | tf_op jit(solution)/shard_map/ppermute | solution.py:38
  58.9 1.0 copy-start.6
  61.9 7.8 %collective-permute-start.2 = (bf16[128,512]{1,0:T(8,128)(2,1)}, bf16[128,512]{1,0:T(8,128)(2,1)S(1)}, u32[]{:S(2)}, u32[]{:S(2)}) collective-permute-start(bf16[128,512]{1,0:T(8,128)(2,1)} %part_sum.2.own_ref), channel_id=1, source_target_pairs={{0,8},{1,9},{2,10},{3,11},{4,12},{5,13},{6,14},{7,15},{8,0},{9,1},... | collective-permute-start | bytes 393224 | tf_op jit(solution)/shard_map/ppermute | solution.py:43
  69.6 0.7 copy-start.7
  72.4 53.4 %all-to-all-start.1 = ((bf16[8,128,512]{2,1,0:T(8,128)(2,1)}), bf16[8,128,512]{2,1,0:T(8,128)(2,1)S(1)}, u32[]{:S(2)}, u32[]{:S(2)}) async-start(bf16[8,128,512]{2,1,0:T(8,128)(2,1)} %masked_sum.2), calls=%async_computation.1 | async-start | bytes 2097152 | tf_op jit(solution)/shard_map/all_to_all | solution.py:21
  77.6 29.8 %collective-permute-start.5 = (bf16[4096,128]{1,0:T(8,128)(2,1)}, bf16[4096,128]{1,0:T(8,128)(2,1)S(1)}, u32[]{:S(2)}, u32[]{:S(2)}) collective-permute-start(bf16[4096,128]{1,0:T(8,128)(2,1)} %get-tuple-element.45), channel_id=1, source_target_pairs={{64,0},{65,1},{66,2},{67,3},{68,4},{69,5},{70,6},{71,7},{72,8},{73... | collective-permute-start | bytes 3145736 | tf_op jit(solution)/shard_map/ppermute | solution.py:38
  78.9 41.5 %collective-permute-start.4 = (bf16[4096,128]{1,0:T(8,128)(2,1)}, bf16[4096,128]{1,0:T(8,128)(2,1)}, u32[]{:S(2)}, u32[]{:S(2)}) collective-permute-start(bf16[4096,128]{1,0:T(8,128)(2,1)} %get-tuple-element.30), channel_id=1, source_target_pairs={{48,0},{49,1},{50,2},{51,3},{52,4},{53,5},{54,6},{55,7},{56,8},{57... | collective-permute-start | bytes 3145736 | tf_op jit(solution)/shard_map/ppermute | solution.py:38
  80.2 45.7 %collective-permute-start.7 = (bf16[4096,128]{1,0:T(8,128)(2,1)}, bf16[4096,128]{1,0:T(8,128)(2,1)}, u32[]{:S(2)}, u32[]{:S(2)}) collective-permute-start(bf16[4096,128]{1,0:T(8,128)(2,1)} %get-tuple-element.32), channel_id=1, source_target_pairs={{80,0},{81,1},{82,2},{83,3},{84,4},{85,5},{86,6},{87,7},{88,8},{89... | collective-permute-start | bytes 3145736 | tf_op jit(solution)/shard_map/ppermute | solution.py:38
  107.4 1.0 copy-start.1
  108.3 12.0 %collective-permute-start.8 = (bf16[2048,128]{1,0:T(8,128)(2,1)}, bf16[2048,128]{1,0:T(8,128)(2,1)}, u32[]{:S(2)}, u32[]{:S(2)}) collective-permute-start(bf16[2048,128]{1,0:T(8,128)(2,1)} %bitcast.23), channel_id=1, source_target_pairs={{128,0},{129,1},{130,2},{131,3},{132,4},{133,5},{134,6},{135,7},{1... | collective-permute-start | bytes 1572872 | tf_op jit(solution)/shard_map/ppermute | solution.py:38
  125.9 1.2 copy-start.2
  127.1 1.0 copy-start.4
  128.1 45.1 %copy-start.10 = (bf16[1,128,128]{2,1,0:T(8,128)(2,1)S(1)}, bf16[1,128,128]{2,1,0:T(8,128)(2,1)}, u32[]{:S(2)}) copy-start(bf16[1,128,128]{2,1,0:T(8,128)(2,1)} %param.13) | copy-start | bytes 98308
  172.4 6.3 %collective-permute-start.9 = (bf16[2,128,128]{2,1,0:T(8,128)(2,1)}, bf16[2,128,128]{2,1,0:T(8,128)(2,1)S(1)}, u32[]{:S(2)}, u32[]{:S(2)}) collective-permute-start(bf16[2,128,128]{2,1,0:T(8,128)(2,1)} %get-tuple-element.38), channel_id=1, source_target_pairs={{0,8},{1,9},{2,10},{3,11},{4,12},{5,13},{6,14},{7,15},{8,0},{9,1},... | collective-permute-start | bytes 196616 | tf_op jit(solution)/shard_map/ppermute | solution.py:43
  173.2 5.5 %collective-permute-start.10 = (bf16[128,128]{1,0:T(8,128)(2,1)S(1)}, bf16[128,128]{1,0:T(8,128)(2,1)S(1)}, u32[]{:S(2)}, u32[]{:S(2)}) collective-permute-start(bf16[128,128]{1,0:T(8,128)(2,1)S(1)} %bitcast.35), channel_id=1, source_target_pairs={{0,8},{1,9},{2,10},{3,11},{4,12},{5,13},{6,14},{7,15},{8,0},{9,1},... | collective-permute-start | bytes 98312 | tf_op jit(solution)/shard_map/ppermute | solution.py:43
  178.7 0.6 copy-start.11
  178.7 0.6 copy-start.9
  195.5 1.2 copy-start.3
  196.8 1.0 copy-start.5
  244.0 6.7 %collective-permute-start.11 = (bf16[128,512]{1,0:T(8,128)(2,1)}, bf16[128,512]{1,0:T(8,128)(2,1)S(1)}, u32[]{:S(2)}, u32[]{:S(2)}) collective-permute-start(bf16[128,512]{1,0:T(8,128)(2,1)} %part_sum.3.own_ref), channel_id=1, source_target_pairs={{0,8},{1,9},{2,10},{3,11},{4,12},{5,13},{6,14},{7,15},{8,0},{9,1},... | collective-permute-start | bytes 393224 | tf_op jit(solution)/shard_map/ppermute | solution.py:43
  250.6 0.7 copy-start.8

commit v3 on v2

--- a/solution.py
+++ b/solution.py
@@ -11,6 +11,7 @@
 BF16 = jnp.bfloat16
 F32 = jnp.float32
 HALVES = 2
+OPERANDS = (2, 6, 1, 3, 4, 5, 7, 8)
 SMEM = pltpu.MemorySpace.SMEM
 VMEM_LIMIT = 40 * 1024 * 1024
 
@@ -86,14 +87,7 @@
 def masked_sum_kernel(own_ref, came_ref, bias_ref, blocks_ref, out_ref):
     tokens, columns = own_ref.shape
     total = own_ref[...].astype(F32) + came_ref[...].astype(F32) + bias_ref[...]
-    blocks = blocks_ref[...].astype(F32)
-    mask = jnp.concatenate(
-        [
-            jnp.broadcast_to(blocks[:, b : b + 1], (tokens, FBLK))
-            for b in range(columns // FBLK)
-        ],
-        axis=1,
-    )
+    mask = spread_mask(blocks_ref[...])
     value = (mask * total).astype(BF16)
     for part in range(out_ref.shape[0]):
         out_ref[part] = value
@@ -107,6 +101,31 @@
     )(own, came, bias, blocks)
 
 
+def spread_mask(blocks):
+    tokens, count = blocks.shape
+    blocks = blocks.astype(F32)
+    return jnp.concatenate(
+        [jnp.broadcast_to(blocks[:, b : b + 1], (tokens, FBLK)) for b in range(count)], axis=1
+    )
+
+
+def masked_total_kernel(parts_ref, blocks_ref, out_ref):
+    total = parts_ref[0].astype(F32)
+    for part in range(1, parts_ref.shape[0]):
+        total = total + parts_ref[part].astype(F32)
+    value = (spread_mask(blocks_ref[...]) * total).astype(BF16)
+    for part in range(out_ref.shape[0]):
+        out_ref[part] = value
+
+
+def masked_total(parts, blocks):
+    return pl.pallas_call(
+        masked_total_kernel,
+        out_shape=jax.ShapeDtypeStruct(parts.shape, BF16),
+        name="masked_total",
+    )(parts, blocks)
+
+
 def summed_over_width(parts, bias, blocks):
     own = part_sum(exchange(parts, "width", HALVES))
     return exchange(masked_sum(own, other_half(own), bias, blocks, parts.shape[0]), "width", HALVES)
@@ -115,26 +134,25 @@
 def weight_specs(near_shape, far_shape, chunk):
     slots, features, cols = near_shape
     far_chunks = far_shape[0] // chunk
-    specs = [pl.BlockSpec((slots, chunk, cols), lambda c, *_: (0, c, 0))]
-    specs += [pl.BlockSpec((chunk, cols), lambda c, *_: (c, 0))] * (slots - 1)
-    specs += [
-        pl.BlockSpec((chunk, cols), lambda c, *_: (jnp.minimum(c, far_chunks - 1), 0)),
-        pl.BlockSpec((chunk, cols), lambda c, *_: (jnp.maximum(c - far_chunks, 0), 0)),
-    ]
-    return specs
-
-
-def decoders_up(step, near_ref, moved_refs, far_ref, far_moved_ref, far_chunks):
+    whole = pl.BlockSpec((chunk, cols), lambda c, *_: (c, 0))
+    lower = pl.BlockSpec((chunk, cols), lambda c, *_: (jnp.minimum(c, far_chunks - 1), 0))
+    upper = pl.BlockSpec((chunk, cols), lambda c, *_: (jnp.maximum(c - far_chunks, 0), 0))
+    near = pl.BlockSpec((slots, chunk, cols), lambda c, *_: (0, c, 0))
+    return [near, lower] + [upper if o == slots else whole for o in OPERANDS]
+
+
+def decoders_up(step, near_ref, far_ref, moved_refs, far_chunks):
     slots = near_ref.shape[0]
-    found = [near_ref[0]] + [ref[...] for ref in moved_refs]
-    found.append(jnp.where(step < far_chunks, far_ref[...], far_moved_ref[...]))
+    moved = dict(zip(OPERANDS, moved_refs))
+    found = [near_ref[0]] + [moved[o][...] for o in range(1, slots)]
+    found.append(jnp.where(step < far_chunks, far_ref[...], moved[slots][...]))
     found += [near_ref[2 * slots - r] for r in range(slots + 1, 2 * slots)]
     return found
 
 
-def forward_kernel(far_chunks, place_ref, acts_ref, near_ref, *refs):
+def forward_kernel(far_chunks, place_ref, acts_ref, near_ref, far_ref, *refs):
     slots = near_ref.shape[0]
-    moved_refs, (far_ref, far_moved_ref, out_ref, total_ref) = refs[: slots - 1], refs[slots - 1 :]
+    moved_refs, (out_ref, total_ref) = refs[:slots], refs[slots:]
     step = pl.program_id(0)
     layers = 2 * slots
     cols = near_ref.shape[2]
@@ -144,7 +162,7 @@
         total_ref[...] = jnp.zeros_like(total_ref)
 
     acts = jnp.concatenate([acts_ref[p] for p in range(acts_ref.shape[0])], axis=1)
-    weights = decoders_up(step, near_ref, moved_refs, far_ref, far_moved_ref, far_chunks)
+    weights = decoders_up(step, near_ref, far_ref, moved_refs, far_chunks)
     for pair in range(slots):
         both = jnp.concatenate(weights[2 * pair : 2 * pair + 2], axis=1)
         total_ref[pair] += jnp.dot(acts, both, preferred_element_type=F32)
@@ -158,7 +176,7 @@
             out_ref[lax.rem(place + r, layers)] = kept.astype(BF16)
 
 
-def forward_shares(place, acts, near, moved, far, far_moved, chunk=512):
+def forward_shares(place, acts, near, far, moved, chunk=512):
     slots, features, cols = near.shape
     parts, tokens, columns = acts.shape
     layers = 2 * slots
@@ -175,7 +193,7 @@
         scratch_shapes=[pltpu.VMEM((slots, tokens, 2 * cols), F32)],
         compiler_params=pltpu.CompilerParams(vmem_limit_bytes=VMEM_LIMIT),
         name="forward_shares",
-    )(place, acts, near, *moved, far, far_moved)
+    )(place, acts, near, far, *moved)
 
 
 def share_sums_kernel(place_ref, shares_ref, own_ref, other_ref, sent_ref):
@@ -234,9 +252,9 @@
     )(place, own, other, came, target, away_target)
 
 
-def backward_kernel(far_chunks, place_ref, grads_ref, near_ref, *refs):
+def backward_kernel(far_chunks, place_ref, grads_ref, near_ref, far_ref, *refs):
     slots = near_ref.shape[0]
-    moved_refs, (far_ref, far_moved_ref, out_ref, up_ref) = refs[: slots - 1], refs[slots - 1 :]
+    moved_refs, (out_ref, up_ref) = refs[:slots], refs[slots:]
     step = pl.program_id(0)
     layers = 2 * slots
     cols = near_ref.shape[2]
@@ -251,7 +269,7 @@
                 place + r < layers, grad, jnp.zeros_like(grad)
             )
 
-    weights = decoders_up(step, near_ref, moved_refs, far_ref, far_moved_ref, far_chunks)
+    weights = decoders_up(step, near_ref, far_ref, moved_refs, far_chunks)
     product = lax.dot_general(
         up_ref[...],
         jnp.concatenate(weights, axis=1),
@@ -262,7 +280,7 @@
         out_ref[part] = product[:, part * columns : (part + 1) * columns].astype(BF16)
 
 
-def backward_parts(place, grads, near, moved, far, far_moved, parts, chunk=512):
+def backward_parts(place, grads, near, far, moved, parts, chunk=512):
     slots, features, cols = near.shape
     layers, tokens, _ = grads.shape
     columns = features // parts
@@ -279,7 +297,7 @@
         scratch_shapes=[pltpu.VMEM((tokens, layers * cols), BF16)],
         compiler_params=pltpu.CompilerParams(vmem_limit_bytes=VMEM_LIMIT),
         name="backward_parts",
-    )(place, grads, near, *moved, far, far_moved)
+    )(place, grads, near, far, *moved)
 
 
 def encoder_grad_kernel(in_ref, pre_ref, enc_ref, bias_ref):
@@ -296,7 +314,7 @@
 def encoder_grads(local_in, pre_grad):
     tokens, rows = local_in.shape
     parts, _, columns = pre_grad.shape
-    step = 2
+    step = 4
     return pl.pallas_call(
         encoder_grad_kernel,
         grid=(parts // step,),
@@ -316,8 +334,8 @@
     )(local_in, pre_grad)
 
 
-FIRST = (1, 7)
-LANES = ((2, 3), (6, 5), (4, 8))
+TARGET = 0
+LANES = ((4, 2), (3, 6), (5, 1), (7, 8, 0))
 
 
 def on_device(inputs, encoder, enc_bias, active_blocks, near_decoders, far_decoders, targets):
@@ -332,32 +350,43 @@
     blocks = lax.dynamic_slice_in_dim(active_blocks[0], column * per_part, per_part, 1)
     bias = lax.dynamic_slice_in_dim(enc_bias, column * columns, columns, 1)
 
-    first = [near[o] for o in FIRST]
+    first = [near[lane[0]] for lane in LANES]
     first, rest, local_in = lax.optimization_barrier((first, near, local_in))
-    moved = {o: shifted_down(slot, o) for o, slot in zip(FIRST, first)}
-    parted = pre_parts(local_in, encoder[0], parts)
-    parted, early = lax.optimization_barrier((parted, [moved[o] for o in FIRST]))
-    moved.update(zip(FIRST, early))
-    for lane in LANES:
+    moved = {}
+    away_target = targets[0]
+    for lane, slot in zip(LANES, first):
         before = None
         for o in lane:
-            slot = far if o == slots else rest[o]
-            if before:
-                slot, moved[before] = lax.optimization_barrier((slot, moved[before]))
-            moved[o] = shifted_down(slot, o)
+            if before is None:
+                moved[o] = shifted_down(slot, o)
+            elif o == TARGET:
+                away_target, moved[before] = lax.optimization_barrier((away_target, moved[before]))
+                away_target = other_half(away_target)
+            else:
+                slot, moved[before] = lax.optimization_barrier(
+                    (far if o == slots else rest[o], moved[before])
+                )
+                moved[o] = shifted_down(slot, o)
             before = o
-    far_moved = moved[slots]
+    parted = pre_parts(local_in, encoder[0], parts)
 
     acts = summed_over_width(parted, bias, blocks)
-    moved = [moved[o] for o in range(1, slots)]
-    shares = forward_shares(place, acts, near, moved, far, far_moved)
+    moved = [moved[o] for o in OPERANDS]
+    shares = forward_shares(place, acts, near, far, moved)
+    shares, away_target = lax.optimization_barrier((shares, away_target))
     own, other, sent = share_sums(place, exchange(shares, "blk"))
     reconstruction, own_grads = residual(
-        place, own, other, other_half(sent), targets[0], other_half(targets[0])
+        place, own, other, other_half(sent), targets[0], away_target
     )
     all_grads = exchange(own_grads, "blk")
-    grad_parts = backward_parts(place, all_grads, near, moved, far, far_moved, parts)
-    pre_grad = summed_over_width(grad_parts, jnp.zeros_like(bias), blocks)
+    all_parts = lax.axis_size("width")
+    grad_parts = backward_parts(place, all_grads, near, far, moved, all_parts)
+    few = active_blocks.shape[2] // all_parts
+    own_blocks = lax.dynamic_slice_in_dim(
+        active_blocks[0], lax.axis_index("width") * few, few, 1
+    )
+    pre_part = masked_total(exchange(grad_parts, "width"), own_blocks)
+    pre_grad = exchange(pre_part, "width")
     enc_grad, bias_grad = encoder_grads(local_in, pre_grad)
     return reconstruction[None], enc_grad[None], bias_grad
 

time: 292 us -> 267 us (0.914); the launches traced: 287 us -> 266 us
  blocking collectives: 112 us -> 73.9 us
  waiting for transfers between devices: 84.3 us -> 94 us
  starting transfers between devices: 33.8 us -> 41.3 us
    all_to_all x4 -> x3, blocking collectives: 112 us -> 73.9 us  [exchange(): lax.all_to_all(parts, axis, 0, 0, tiled=True, axis_index_groups=groups)]
    all_to_all x2 -> x3, waiting for transfers between devices: 20.4 us -> 48.8 us  [exchange(): lax.all_to_all(parts, axis, 0, 0, tiled=True, axis_index_groups=groups)]
    ppermute x8, waiting for transfers between devices: 54.9 us -> 39.7 us  [shifted_down(): return lax.ppermute(block, ('blk', 'width'), route)]
    all_to_all x2 -> x3, starting transfers between devices: 13.7 us -> 22.6 us  [exchange(): lax.all_to_all(parts, axis, 0, 0, tiled=True, axis_index_groups=groups)]
    ppermute x4 -> x3, waiting for transfers between devices: 8.94 us -> 5.47 us  [other_half(): lax.ppermute(block, 'width', [(p, (p + parts // 2) % parts) for p in rang...]
    ppermute x4 -> x3, starting transfers between devices: 9.84 us -> 8.39 us  [other_half(): lax.ppermute(block, 'width', [(p, (p + parts // 2) % parts) for p in rang...]
  transfers between devices with their start and end apart: 14 -> 14, of which waited for: 8 -> 6; matrix products, arithmetic and copies ran while one was open for 2% -> 2% of each run, Pallas kernels for 3% -> 5%
where the time goes in v3:
time: 267 us; the launch traced here: 266 us
  waiting for transfers between devices  94 us (35%)
  blocking collectives  73.9 us (28%)
  starting transfers between devices  41.3 us (15%)
  Pallas kernels  37.1 us (14%)
  local copies, waits for them, and re-layouts  18.8 us (7%)
    all_to_all x3, blocking collectives, exchange(): lax.all_to_all(parts, axis, 0, 0, tiled=True, axis_index_groups=groups)  73.9 us
    all_to_all x3, waiting for transfers between devices, exchange(): lax.all_to_all(parts, axis, 0, 0, tiled=True, axis_index_groups=groups)  48.8 us
    ppermute x8, waiting for transfers between devices, shifted_down(): return lax.ppermute(block, ('blk', 'width'), route)  39.7 us
    all_to_all x3, starting transfers between devices, exchange(): lax.all_to_all(parts, axis, 0, 0, tiled=True, axis_index_groups=groups)  22.6 us
    pallas_call x1, Pallas kernels, backward_parts(): pl.pallas_call(functools.partial(backward_kernel, far.shape[0] // chunk),...  11 us
    ppermute x8, starting transfers between devices, shifted_down(): return lax.ppermute(block, ('blk', 'width'), route)  10.3 us
    pallas_call x1, Pallas kernels, forward_shares(): pl.pallas_call(functools.partial(forward_kernel, far.shape[0] // chunk),...  8.42 us
    ppermute x3, starting transfers between devices, other_half(): lax.ppermute(block, 'width', [(p, (p + parts // 2) % parts) for p in rang...  8.39 us
  transfers between devices with their start and end apart: 14, of which 6 were waited for; matrix products, arithmetic and copies ran while one was open for 2% of the time, Pallas kernels for 5%

profile of v3, /device:TPU:32, one launch (start us, length us, event | category | flops | bytes accessed | tf_op | source)
XLA Modules:
  0.0 265.9 jit_solution(1090898149739565451)
XLA Ops:
  0.6 4.2 %slice_bitcast_fusion.3 = (bf16[4096,128]{1,0:T(8,128)(2,1)}, bf16[4096,128]{1,0:T(8,128)(2,1)}, bf16[4096,128]{1,0:T(8,128)(2,1)}, bf16[4096,128]{1,0:T(8,128)(2,1)}) fusion(bf16[1,8,4096,128]{3,2,1,0:T(8,128)(2,1)} %param.11), kind=kLoop, calls=%fused_computation.3 | loop fusion | bytes 8388608 | tf_op jit(solution)/shard_map/squeeze | solution.py:353
  4.9 3.8 %pre_parts.1 = bf16[8,128,512]{2,1,0:T(8,128)(2,1)} custom-call(bf16[128,128]{1,0:T(8,128)(2,1)} %bitcast.33, bf16[128,4096]{1,0:T(8,128)(2,1)} %bitcast.30), custom_call_target="tpu_custom_call" | custom-call | tf_op jit(solution)/shard_map/pre_parts/pallas_call | solution.py:59
  8.6 8.6 %all-to-all-start = ((bf16[8,128,512]{2,1,0:T(8,128)(2,1)}), bf16[8,128,512]{2,1,0:T(8,128)(2,1)S(1)}, u32[]{:S(2)}, u32[]{:S(2)}) async-start(bf16[8,128,512]{2,1,0:T(8,128)(2,1)} %pre_parts.1), calls=%async_computation | async-start | bytes 2097152 | tf_op jit(solution)/shard_map/all_to_all | solution.py:22
  18.5 1.3 collective-permute-start.3
  19.8 1.3 collective-permute-start.5
  21.1 1.3 collective-permute-start.7
  22.4 22.1 %all-to-all-done.parts_ref = bf16[8,128,512]{2,1,0:T(8,128)(2,1)S(1)} async-done(((bf16[8,128,512]{2,1,0:T(8,128)(2,1)}), bf16[8,128,512]{2,1,0:T(8,128)(2,1)S(1)}, u32[]{:S(2)}, u32[]{:S(2)}) %all-to-all-start) | async-done | bytes 1048608 | tf_op jit(solution)/shard_map/all_to_all | solution.py:22
  45.5 2.0 part_sum.1.own_ref
  47.5 3.2 %collective-permute-start = (bf16[128,512]{1,0:T(8,128)(2,1)}, bf16[128,512]{1,0:T(8,128)(2,1)S(1)}, u32[]{:S(2)}, u32[]{:S(2)}) collective-permute-start(bf16[128,512]{1,0:T(8,128)(2,1)} %part_sum.1.own_ref), channel_id=1, source_target_pairs={{0,8},{1,9},{2,10},{3,11},{4,12},{5,13},{6,14},{7,15},{8,0},{9,1},... | collective-permute-start | bytes 393224 | tf_op jit(solution)/shard_map/ppermute | solution.py:44
  52.7 1.5 collective-permute-done.came_ref
  54.8 2.1 masked_sum.1
  56.9 5.4 %all-to-all-start.1 = ((bf16[8,128,512]{2,1,0:T(8,128)(2,1)}), bf16[8,128,512]{2,1,0:T(8,128)(2,1)S(1)}, u32[]{:S(2)}, u32[]{:S(2)}) async-start(bf16[8,128,512]{2,1,0:T(8,128)(2,1)} %masked_sum.1), calls=%async_computation.1 | async-start | bytes 2097152 | tf_op jit(solution)/shard_map/all_to_all | solution.py:22
  62.3 3.6 %slice_bitcast_fusion = (bf16[4096,128]{1,0:T(8,128)(2,1)}, bf16[4096,128]{1,0:T(8,128)(2,1)}, bf16[4096,128]{1,0:T(8,128)(2,1)}) fusion(bf16[8,4096,128]{2,1,0:T(8,128)(2,1)} %bitcast.27), kind=kLoop, calls=%fused_computation | loop fusion | bytes 6291456 | tf_op jit(solution)/shard_map/squeeze | solution.py:367
  65.9 1.3 collective-permute-start.2
  67.2 1.3 collective-permute-start.4
  68.6 1.3 collective-permute-start.6
  69.9 20.4 %collective-permute-done.7.refs_6_ = bf16[4096,128]{1,0:T(8,128)(2,1)} collective-permute-done((bf16[4096,128]{1,0:T(8,128)(2,1)}, bf16[4096,128]{1,0:T(8,128)(2,1)}, u32[]{:S(2)}, u32[]{:S(2)}) %collective-permute-start.7) | collective-permute-done | bytes 1048608 | tf_op jit(solution)/shard_map/ppermute | solution.py:39
  91.6 19.2 %collective-permute-done.8.refs_7_ = bf16[2048,128]{1,0:T(8,128)(2,1)S(1)} collective-permute-done((bf16[2048,128]{1,0:T(8,128)(2,1)}, bf16[2048,128]{1,0:T(8,128)(2,1)S(1)}, u32[]{:S(2)}, u32[]{:S(2)}) %collective-permute-start.8) | collective-permute-done | bytes 524320 | tf_op jit(solution)/shard_map/ppermute | solution.py:39
  111.6 3.2 %collective-permute-start.9 = (bf16[128,128]{1,0:T(8,128)(2,1)S(1)}, bf16[128,128]{1,0:T(8,128)(2,1)S(1)}, u32[]{:S(2)}, u32[]{:S(2)}) collective-permute-start(bf16[128,128]{1,0:T(8,128)(2,1)S(1)} %bitcast.36), channel_id=1, source_target_pairs={{0,8},{1,9},{2,10},{3,11},{4,12},{5,13},{6,14},{7,15},{8,0},{9,1},... | collective-permute-start | bytes 98312 | tf_op jit(solution)/shard_map/ppermute | solution.py:44
  116.9 8.4 %forward_shares.1 = bf16[16,128,128]{2,1,0:T(8,128)(2,1)S(1)} custom-call(s32[1]{0:T(128)} %bitcast.place_ref, bf16[8,128,512]{2,1,0:T(8,128)(2,1)S(1)} %all-to-all-done.1.acts_ref, bf16[8,4096,128]{2,1,0:T(8,128)(2,1)} %bitcast.28, bf16[2048,128]{1,0:T(8,128)(2,1)S(1)} %bitcast.25, bf16[4096,128]{1,0:T(8,128)(2,1)} %collective-permute-done.2.refs_0_, ...), custom_call_target="tpu_custom_call" | custom-call | tf_op jit(solution)/shard_map/forward_shares/pallas_call | solution.py:183
  125.4 26.7 %all_to_all.30.shares_ref = bf16[16,128,128]{2,1,0:T(8,128)(2,1)} all-to-all(bf16[16,128,128]{2,1,0:T(8,128)(2,1)S(1)} %forward_shares.1), channel_id=1, replica_groups={{0,16,32,48,64,80,96,112,128,144,160,176,192,208,224,240},{1,17,33,49,6..., dimensions={0} | all-to-all | bytes 1048576 | tf_op jit(solution)/shard_map/all_to_all | solution.py:22
  152.0 1.8 share_sums.1
  153.8 2.0 collective-permute-start.10
  155.8 4.0 %collective-permute-done.10.came_ref = bf16[2,128,128]{2,1,0:T(8,128)(2,1)S(1)} collective-permute-done((bf16[2,128,128]{2,1,0:T(8,128)(2,1)}, bf16[2,128,128]{2,1,0:T(8,128)(2,1)S(1)}, u32[]{:S(2)}, u32[]{:S(2)}) %collective-permute-start.10) | collective-permute-done | bytes 65568 | tf_op jit(solution)/shard_map/ppermute | solution.py:44
  160.4 1.8 residual.1
  162.2 14.4 %all_to_all.31.grads_ref = bf16[16,128,128]{2,1,0:T(8,128)(2,1)S(1)} all-to-all(bf16[16,128,128]{2,1,0:T(8,128)(2,1)} %get-tuple-element.50), channel_id=1, replica_groups={{0,16,32,48,64,80,96,112,128,144,160,176,192,208,224,240},{1,17,33,49,6..., dimensions={0} | all-to-all | bytes 1048576 | tf_op jit(solution)/shard_map/all_to_all | solution.py:22
  178.7 11.0 %backward_parts.1 = bf16[16,128,256]{2,1,0:T(8,128)(2,1)} custom-call(s32[1]{0:T(128)} %bitcast.place_ref, bf16[16,128,128]{2,1,0:T(8,128)(2,1)S(1)} %all_to_all.31.grads_ref, bf16[8,4096,128]{2,1,0:T(8,128)(2,1)} %bitcast.29, bf16[2048,128]{1,0:T(8,128)(2,1)S(1)} %bitcast.26, bf16[4096,128]{1,0:T(8,128)(2,1)} %collective-permute-done.2.refs_0_, ...), custom_call_target="tpu_custom_call" | custom-call | tf_op jit(solution)/shard_map/backward_parts/pallas_call | solution.py:287
  189.6 8.7 %all-to-all-start.4 = ((bf16[16,128,256]{2,1,0:T(8,128)(2,1)}), bf16[16,128,256]{2,1,0:T(8,128)(2,1)S(1)}, u32[]{:S(2)}, u32[]{:S(2)}) async-start(bf16[16,128,256]{2,1,0:T(8,128)(2,1)} %backward_parts.1), calls=%async_computation.4 | async-start | bytes 2097152 | tf_op jit(solution)/shard_map/all_to_all | solution.py:22
  199.1 26.8 %all-to-all-done.4.parts_ref = bf16[16,128,256]{2,1,0:T(8,128)(2,1)S(1)} async-done(((bf16[16,128,256]{2,1,0:T(8,128)(2,1)}), bf16[16,128,256]{2,1,0:T(8,128)(2,1)S(1)}, u32[]{:S(2)}, u32[]{:S(2)}) %all-to-all-start.4) | async-done | bytes 1048608 | tf_op jit(solution)/shard_map/all_to_all | solution.py:22
  226.8 2.4 masked_total.1
  229.2 32.9 %all_to_all.32.pre_ref = bf16[16,128,256]{2,1,0:T(8,128)(2,1)} all-to-all(bf16[16,128,256]{2,1,0:T(8,128)(2,1)} %masked_total.1), channel_id=1, replica_groups={{0,1,2,3,4,5,6,7,8,9,10,11,12,13,14,15},{16,17,18,19,20,21,22,23,24,25,..., dimensions={0} | all-to-all | bytes 2097152 | tf_op jit(solution)/shard_map/all_to_all | solution.py:22
  262.1 3.8 %encoder_grads.1 = (bf16[128,4096]{1,0:T(8,128)(2,1)}, f32[1,4096]{1,0:T(1,128)}) custom-call(bf16[128,128]{1,0:T(8,128)(2,1)} %bitcast.34, bf16[16,128,256]{2,1,0:T(8,128)(2,1)} %all_to_all.32.pre_ref), custom_call_target="tpu_custom_call" | custom-call | tf_op jit(solution)/shard_map/encoder_grads/pallas_call | solution.py:318
  (39 shorter events, 13.5 us)
Async XLA Ops:
  0.6 51.3 %copy-start = (s32[1,128,32]{1,2,0:T(8,128)S(1)}, s32[1,128,32]{1,2,0:T(8,128)}, u32[]{:S(2)}) copy-start(s32[1,128,32]{1,2,0:T(8,128)} %param.10) | copy-start | bytes 49156
  4.9 106.7 %copy-start.10 = (bf16[1,128,128]{2,1,0:T(8,128)(2,1)S(1)}, bf16[1,128,128]{2,1,0:T(8,128)(2,1)}, u32[]{:S(2)}) copy-start(bf16[1,128,128]{2,1,0:T(8,128)(2,1)} %param.13) | copy-start | bytes 98308
  8.6 35.8 %all-to-all-start = ((bf16[8,128,512]{2,1,0:T(8,128)(2,1)}), bf16[8,128,512]{2,1,0:T(8,128)(2,1)S(1)}, u32[]{:S(2)}, u32[]{:S(2)}) async-start(bf16[8,128,512]{2,1,0:T(8,128)(2,1)} %pre_parts.1), calls=%async_computation | async-start | bytes 2097152 | tf_op jit(solution)/shard_map/all_to_all | solution.py:22
  17.2 48.7 %collective-permute-start.1 = (bf16[4096,128]{1,0:T(8,128)(2,1)}, bf16[4096,128]{1,0:T(8,128)(2,1)S(1)}, u32[]{:S(2)}, u32[]{:S(2)}) collective-permute-start(bf16[4096,128]{1,0:T(8,128)(2,1)} %get-tuple-element.30), channel_id=1, source_target_pairs={{64,0},{65,1},{66,2},{67,3},{68,4},{69,5},{70,6},{71,7},{72,8},{73... | collective-permute-start | bytes 3145736 | tf_op jit(solution)/shard_map/ppermute | solution.py:39
  18.5 48.7 %collective-permute-start.3 = (bf16[4096,128]{1,0:T(8,128)(2,1)}, bf16[4096,128]{1,0:T(8,128)(2,1)S(1)}, u32[]{:S(2)}, u32[]{:S(2)}) collective-permute-start(bf16[4096,128]{1,0:T(8,128)(2,1)} %get-tuple-element.32), channel_id=1, source_target_pairs={{48,0},{49,1},{50,2},{51,3},{52,4},{53,5},{54,6},{55,7},{56,8},{57... | collective-permute-start | bytes 3145736 | tf_op jit(solution)/shard_map/ppermute | solution.py:39
  19.8 48.7 %collective-permute-start.5 = (bf16[4096,128]{1,0:T(8,128)(2,1)}, bf16[4096,128]{1,0:T(8,128)(2,1)}, u32[]{:S(2)}, u32[]{:S(2)}) collective-permute-start(bf16[4096,128]{1,0:T(8,128)(2,1)} %get-tuple-element.34), channel_id=1, source_target_pairs={{80,0},{81,1},{82,2},{83,3},{84,4},{85,5},{86,6},{87,7},{88,8},{89... | collective-permute-start | bytes 3145736 | tf_op jit(solution)/shard_map/ppermute | solution.py:39
  21.1 69.2 %collective-permute-start.7 = (bf16[4096,128]{1,0:T(8,128)(2,1)}, bf16[4096,128]{1,0:T(8,128)(2,1)}, u32[]{:S(2)}, u32[]{:S(2)}) collective-permute-start(bf16[4096,128]{1,0:T(8,128)(2,1)} %get-tuple-element.39), channel_id=1, source_target_pairs={{112,0},{113,1},{114,2},{115,3},{116,4},{117,5},{118,6},{119,7},{1... | collective-permute-start | bytes 3145736 | tf_op jit(solution)/shard_map/ppermute | solution.py:39
  44.5 1.0 copy-start.6
  47.5 6.7 %collective-permute-start = (bf16[128,512]{1,0:T(8,128)(2,1)}, bf16[128,512]{1,0:T(8,128)(2,1)S(1)}, u32[]{:S(2)}, u32[]{:S(2)}) collective-permute-start(bf16[128,512]{1,0:T(8,128)(2,1)} %part_sum.1.own_ref), channel_id=1, source_target_pairs={{0,8},{1,9},{2,10},{3,11},{4,12},{5,13},{6,14},{7,15},{8,0},{9,1},... | collective-permute-start | bytes 393224 | tf_op jit(solution)/shard_map/ppermute | solution.py:44
  54.1 0.7 copy-start.8
  56.9 57.9 %all-to-all-start.1 = ((bf16[8,128,512]{2,1,0:T(8,128)(2,1)}), bf16[8,128,512]{2,1,0:T(8,128)(2,1)S(1)}, u32[]{:S(2)}, u32[]{:S(2)}) async-start(bf16[8,128,512]{2,1,0:T(8,128)(2,1)} %masked_sum.1), calls=%async_computation.1 | async-start | bytes 2097152 | tf_op jit(solution)/shard_map/all_to_all | solution.py:22
  65.9 48.8 %collective-permute-start.2 = (bf16[4096,128]{1,0:T(8,128)(2,1)}, bf16[4096,128]{1,0:T(8,128)(2,1)}, u32[]{:S(2)}, u32[]{:S(2)}) collective-permute-start(bf16[4096,128]{1,0:T(8,128)(2,1)} %get-tuple-element.31), channel_id=1, source_target_pairs={{32,0},{33,1},{34,2},{35,3},{36,4},{37,5},{38,6},{39,7},{40,8},{41... | collective-permute-start | bytes 3145736 | tf_op jit(solution)/shard_map/ppermute | solution.py:39
  67.2 47.6 %collective-permute-start.4 = (bf16[4096,128]{1,0:T(8,128)(2,1)}, bf16[4096,128]{1,0:T(8,128)(2,1)}, u32[]{:S(2)}, u32[]{:S(2)}) collective-permute-start(bf16[4096,128]{1,0:T(8,128)(2,1)} %get-tuple-element.33), channel_id=1, source_target_pairs={{96,0},{97,1},{98,2},{99,3},{100,4},{101,5},{102,6},{103,7},{104,8... | collective-permute-start | bytes 3145736 | tf_op jit(solution)/shard_map/ppermute | solution.py:39
  68.6 46.2 %collective-permute-start.6 = (bf16[4096,128]{1,0:T(8,128)(2,1)}, bf16[4096,128]{1,0:T(8,128)(2,1)}, u32[]{:S(2)}, u32[]{:S(2)}) collective-permute-start(bf16[4096,128]{1,0:T(8,128)(2,1)} %get-tuple-element.35), channel_id=1, source_target_pairs={{16,0},{17,1},{18,2},{19,3},{20,4},{21,5},{22,6},{23,7},{24,8},{25... | collective-permute-start | bytes 3145736 | tf_op jit(solution)/shard_map/ppermute | solution.py:39
  90.3 20.5 %collective-permute-start.8 = (bf16[2048,128]{1,0:T(8,128)(2,1)}, bf16[2048,128]{1,0:T(8,128)(2,1)S(1)}, u32[]{:S(2)}, u32[]{:S(2)}) collective-permute-start(bf16[2048,128]{1,0:T(8,128)(2,1)} %bitcast.24), channel_id=1, source_target_pairs={{128,0},{129,1},{130,2},{131,3},{132,4},{133,5},{134,6},{135,7},{1... | collective-permute-start | bytes 1572872 | tf_op jit(solution)/shard_map/ppermute | solution.py:39
  110.8 0.8 copy-start.3
  111.6 13.7 %collective-permute-start.9 = (bf16[128,128]{1,0:T(8,128)(2,1)S(1)}, bf16[128,128]{1,0:T(8,128)(2,1)S(1)}, u32[]{:S(2)}, u32[]{:S(2)}) collective-permute-start(bf16[128,128]{1,0:T(8,128)(2,1)S(1)} %bitcast.36), channel_id=1, source_target_pairs={{0,8},{1,9},{2,10},{3,11},{4,12},{5,13},{6,14},{7,15},{8,0},{9,1},... | collective-permute-start | bytes 98312 | tf_op jit(solution)/shard_map/ppermute | solution.py:44
  114.8 1.0 copy-start.1
  115.9 1.0 copy-start.4
  125.3 34.4 %copy-start.11 = (bf16[128,128]{1,0:T(8,128)(2,1)}, bf16[128,128]{1,0:T(8,128)(2,1)S(1)}, u32[]{:S(2)}) copy-start(bf16[128,128]{1,0:T(8,128)(2,1)S(1)} %collective-permute-done.9.away_target_ref) | copy-start | bytes 98308
  153.8 6.0 %collective-permute-start.10 = (bf16[2,128,128]{2,1,0:T(8,128)(2,1)}, bf16[2,128,128]{2,1,0:T(8,128)(2,1)S(1)}, u32[]{:S(2)}, u32[]{:S(2)}) collective-permute-start(bf16[2,128,128]{2,1,0:T(8,128)(2,1)} %get-tuple-element.47), channel_id=1, source_target_pairs={{0,8},{1,9},{2,10},{3,11},{4,12},{5,13},{6,14},{7,15},{8,0},{9,1},... | collective-permute-start | bytes 196616 | tf_op jit(solution)/shard_map/ppermute | solution.py:44
  159.8 0.6 copy-start.9
  176.6 1.0 copy-start.2
  177.6 1.0 copy-start.5
  189.6 36.2 %all-to-all-start.4 = ((bf16[16,128,256]{2,1,0:T(8,128)(2,1)}), bf16[16,128,256]{2,1,0:T(8,128)(2,1)S(1)}, u32[]{:S(2)}, u32[]{:S(2)}) async-start(bf16[16,128,256]{2,1,0:T(8,128)(2,1)} %backward_parts.1), calls=%async_computation.4 | async-start | bytes 2097152 | tf_op jit(solution)/shard_map/all_to_all | solution.py:22
  225.8 1.0 copy-start.7

commit v4 on v3

--- a/solution.py
+++ b/solution.py
@@ -176,7 +176,7 @@
             out_ref[lax.rem(place + r, layers)] = kept.astype(BF16)
 
 
-def forward_shares(place, acts, near, far, moved, chunk=512):
+def forward_shares(place, acts, near, far, moved, chunk=1024):
     slots, features, cols = near.shape
     parts, tokens, columns = acts.shape
     layers = 2 * slots
@@ -280,7 +280,7 @@
         out_ref[part] = product[:, part * columns : (part + 1) * columns].astype(BF16)
 
 
-def backward_parts(place, grads, near, far, moved, parts, chunk=512):
+def backward_parts(place, grads, near, far, moved, parts, chunk=1024):
     slots, features, cols = near.shape
     layers, tokens, _ = grads.shape
     columns = features // parts
@@ -314,7 +314,7 @@
 def encoder_grads(local_in, pre_grad):
     tokens, rows = local_in.shape
     parts, _, columns = pre_grad.shape
-    step = 4
+    step = 8
     return pl.pallas_call(
         encoder_grad_kernel,
         grid=(parts // step,),
@@ -351,7 +351,7 @@
     bias = lax.dynamic_slice_in_dim(enc_bias, column * columns, columns, 1)
 
     first = [near[lane[0]] for lane in LANES]
-    first, rest, local_in = lax.optimization_barrier((first, near, local_in))
+    first, rest = lax.optimization_barrier((first, near))
     moved = {}
     away_target = targets[0]
     for lane, slot in zip(LANES, first):

time: 267 us -> 262 us (0.981)
  Pallas kernels: 37.1 us -> 32.4 us
    all_to_all x3, waiting for transfers between devices: 48.8 us -> 44.6 us  [exchange(): lax.all_to_all(parts, axis, 0, 0, tiled=True, axis_index_groups=groups)]
    ppermute x8, waiting for transfers between devices: 39.7 us -> 42.3 us  [shifted_down(): return lax.ppermute(block, ('blk', 'width'), route)]
  transfers between devices with their start and end apart: 14 -> 14, of which waited for: 6 -> 7; matrix products, arithmetic and copies ran while one was open for 2% -> 4% of each run, Pallas kernels for 5% -> 4%
where the time goes in v4:
time: 262 us; the launch traced here: 260 us
  waiting for transfers between devices  93 us (35%)
  blocking collectives  73.7 us (28%)
  starting transfers between devices  41.6 us (16%)
  Pallas kernels  32.4 us (12%)
  local copies, waits for them, and re-layouts  18.8 us (7%)
    all_to_all x3, blocking collectives, exchange(): lax.all_to_all(parts, axis, 0, 0, tiled=True, axis_index_groups=groups)  73.7 us
    all_to_all x3, waiting for transfers between devices, exchange(): lax.all_to_all(parts, axis, 0, 0, tiled=True, axis_index_groups=groups)  44.6 us
    ppermute x8, waiting for transfers between devices, shifted_down(): return lax.ppermute(block, ('blk', 'width'), route)  42.3 us
    all_to_all x3, starting transfers between devices, exchange(): lax.all_to_all(parts, axis, 0, 0, tiled=True, axis_index_groups=groups)  21.9 us
    ppermute x8, starting transfers between devices, shifted_down(): return lax.ppermute(block, ('blk', 'width'), route)  10.3 us
    ppermute x3, starting transfers between devices, other_half(): lax.ppermute(block, 'width', [(p, (p + parts // 2) % parts) for p in rang...  9.41 us
    pallas_call x1, Pallas kernels, backward_parts(): pl.pallas_call(functools.partial(backward_kernel, far.shape[0] // chunk),...  9.37 us
    unnamed x24, local copies, waits for them, and re-layouts  8.18 us
  transfers between devices with their start and end apart: 14, of which 7 were waited for; matrix products, arithmetic and copies ran while one was open for 4% of the time, Pallas kernels for 4%

profile of v4, /device:TPU:32, one launch (start us, length us, event | category | flops | bytes accessed | tf_op | source)
XLA Modules:
  0.0 260.4 jit_solution(4167489357419198284)
XLA Ops:
  0.6 3.8 %pre_parts.1 = bf16[8,128,512]{2,1,0:T(8,128)(2,1)} custom-call(bf16[128,128]{1,0:T(8,128)(2,1)} %bitcast.33, bf16[128,4096]{1,0:T(8,128)(2,1)} %bitcast.30), custom_call_target="tpu_custom_call" | custom-call | tf_op jit(solution)/shard_map/pre_parts/pallas_call | solution.py:59
  4.4 8.6 %all-to-all-start = ((bf16[8,128,512]{2,1,0:T(8,128)(2,1)}), bf16[8,128,512]{2,1,0:T(8,128)(2,1)S(1)}, u32[]{:S(2)}, u32[]{:S(2)}) async-start(bf16[8,128,512]{2,1,0:T(8,128)(2,1)} %pre_parts.1), calls=%async_computation | async-start | bytes 2097152 | tf_op jit(solution)/shard_map/all_to_all | solution.py:22
  13.0 4.3 %slice_bitcast_fusion.3 = (bf16[4096,128]{1,0:T(8,128)(2,1)}, bf16[4096,128]{1,0:T(8,128)(2,1)}, bf16[4096,128]{1,0:T(8,128)(2,1)}, bf16[4096,128]{1,0:T(8,128)(2,1)}) fusion(bf16[1,8,4096,128]{3,2,1,0:T(8,128)(2,1)} %param.11), kind=kLoop, calls=%fused_computation.3 | loop fusion | bytes 8388608 | tf_op jit(solution)/shard_map/squeeze | solution.py:353
  18.5 1.3 collective-permute-start.3
  19.8 1.3 collective-permute-start.5
  21.1 1.3 collective-permute-start.7
  22.5 17.8 %all-to-all-done.parts_ref = bf16[8,128,512]{2,1,0:T(8,128)(2,1)S(1)} async-done(((bf16[8,128,512]{2,1,0:T(8,128)(2,1)}), bf16[8,128,512]{2,1,0:T(8,128)(2,1)S(1)}, u32[]{:S(2)}, u32[]{:S(2)}) %all-to-all-start) | async-done | bytes 1048608 | tf_op jit(solution)/shard_map/all_to_all | solution.py:22
  41.2 2.0 part_sum.1.own_ref
  43.2 3.2 %collective-permute-start = (bf16[128,512]{1,0:T(8,128)(2,1)}, bf16[128,512]{1,0:T(8,128)(2,1)S(1)}, u32[]{:S(2)}, u32[]{:S(2)}) collective-permute-start(bf16[128,512]{1,0:T(8,128)(2,1)} %part_sum.1.own_ref), channel_id=1, source_target_pairs={{0,8},{1,9},{2,10},{3,11},{4,12},{5,13},{6,14},{7,15},{8,0},{9,1},... | collective-permute-start | bytes 393224 | tf_op jit(solution)/shard_map/ppermute | solution.py:44
  48.4 1.5 collective-permute-done.came_ref
  50.6 2.1 masked_sum.1
  52.7 5.4 %all-to-all-start.1 = ((bf16[8,128,512]{2,1,0:T(8,128)(2,1)}), bf16[8,128,512]{2,1,0:T(8,128)(2,1)S(1)}, u32[]{:S(2)}, u32[]{:S(2)}) async-start(bf16[8,128,512]{2,1,0:T(8,128)(2,1)} %masked_sum.1), calls=%async_computation.1 | async-start | bytes 2097152 | tf_op jit(solution)/shard_map/all_to_all | solution.py:22
  58.1 3.6 %slice_bitcast_fusion = (bf16[4096,128]{1,0:T(8,128)(2,1)}, bf16[4096,128]{1,0:T(8,128)(2,1)}, bf16[4096,128]{1,0:T(8,128)(2,1)}) fusion(bf16[8,4096,128]{2,1,0:T(8,128)(2,1)} %bitcast.27), kind=kLoop, calls=%fused_computation | loop fusion | bytes 6291456 | tf_op jit(solution)/shard_map/squeeze | solution.py:367
  61.7 1.3 collective-permute-start.2
  63.0 1.3 collective-permute-start.4
  64.3 1.8 collective-permute-done.5.refs_5_
  67.4 22.9 %collective-permute-done.7.refs_6_ = bf16[4096,128]{1,0:T(8,128)(2,1)} collective-permute-done((bf16[4096,128]{1,0:T(8,128)(2,1)}, bf16[4096,128]{1,0:T(8,128)(2,1)}, u32[]{:S(2)}, u32[]{:S(2)}) %collective-permute-start.7) | collective-permute-done | bytes 1048608 | tf_op jit(solution)/shard_map/ppermute | solution.py:39
  91.6 17.6 %collective-permute-done.8.refs_7_ = bf16[2048,128]{1,0:T(8,128)(2,1)S(1)} collective-permute-done((bf16[2048,128]{1,0:T(8,128)(2,1)}, bf16[2048,128]{1,0:T(8,128)(2,1)S(1)}, u32[]{:S(2)}, u32[]{:S(2)}) %collective-permute-start.8) | collective-permute-done | bytes 524320 | tf_op jit(solution)/shard_map/ppermute | solution.py:39
  110.0 4.9 %collective-permute-start.9 = (bf16[128,128]{1,0:T(8,128)(2,1)S(1)}, bf16[128,128]{1,0:T(8,128)(2,1)S(1)}, u32[]{:S(2)}, u32[]{:S(2)}) collective-permute-start(bf16[128,128]{1,0:T(8,128)(2,1)S(1)} %bitcast.36), channel_id=1, source_target_pairs={{0,8},{1,9},{2,10},{3,11},{4,12},{5,13},{6,14},{7,15},{8,0},{9,1},... | collective-permute-start | bytes 98312 | tf_op jit(solution)/shard_map/ppermute | solution.py:44
  117.0 6.7 %forward_shares.1 = bf16[16,128,128]{2,1,0:T(8,128)(2,1)S(1)} custom-call(s32[1]{0:T(128)} %bitcast.place_ref, bf16[8,128,512]{2,1,0:T(8,128)(2,1)S(1)} %all-to-all-done.1.acts_ref, bf16[8,4096,128]{2,1,0:T(8,128)(2,1)} %bitcast.28, bf16[2048,128]{1,0:T(8,128)(2,1)S(1)} %bitcast.25, bf16[4096,128]{1,0:T(8,128)(2,1)} %collective-permute-done.2.refs_0_, ...), custom_call_target="tpu_custom_call" | custom-call | tf_op jit(solution)/shard_map/forward_shares/pallas_call | solution.py:183
  123.7 26.4 %all_to_all.30.shares_ref = bf16[16,128,128]{2,1,0:T(8,128)(2,1)} all-to-all(bf16[16,128,128]{2,1,0:T(8,128)(2,1)S(1)} %forward_shares.1), channel_id=1, replica_groups={{0,16,32,48,64,80,96,112,128,144,160,176,192,208,224,240},{1,17,33,49,6..., dimensions={0} | all-to-all | bytes 1048576 | tf_op jit(solution)/shard_map/all_to_all | solution.py:22
  150.2 1.8 share_sums.1
  152.0 1.3 collective-permute-start.10
  153.3 4.7 %collective-permute-done.10.came_ref = bf16[2,128,128]{2,1,0:T(8,128)(2,1)S(1)} collective-permute-done((bf16[2,128,128]{2,1,0:T(8,128)(2,1)}, bf16[2,128,128]{2,1,0:T(8,128)(2,1)S(1)}, u32[]{:S(2)}, u32[]{:S(2)}) %collective-permute-start.10) | collective-permute-done | bytes 65568 | tf_op jit(solution)/shard_map/ppermute | solution.py:44
  158.6 1.8 residual.1
  160.3 14.4 %all_to_all.31.grads_ref = bf16[16,128,128]{2,1,0:T(8,128)(2,1)S(1)} all-to-all(bf16[16,128,128]{2,1,0:T(8,128)(2,1)} %get-tuple-element.48), channel_id=1, replica_groups={{0,16,32,48,64,80,96,112,128,144,160,176,192,208,224,240},{1,17,33,49,6..., dimensions={0} | all-to-all | bytes 1048576 | tf_op jit(solution)/shard_map/all_to_all | solution.py:22
  176.8 9.4 %backward_parts.1 = bf16[16,128,256]{2,1,0:T(8,128)(2,1)} custom-call(s32[1]{0:T(128)} %bitcast.place_ref, bf16[16,128,128]{2,1,0:T(8,128)(2,1)S(1)} %all_to_all.31.grads_ref, bf16[8,4096,128]{2,1,0:T(8,128)(2,1)} %bitcast.29, bf16[2048,128]{1,0:T(8,128)(2,1)S(1)} %bitcast.26, bf16[4096,128]{1,0:T(8,128)(2,1)} %collective-permute-done.2.refs_0_, ...), custom_call_target="tpu_custom_call" | custom-call | tf_op jit(solution)/shard_map/backward_parts/pallas_call | solution.py:287
  186.2 8.0 %all-to-all-start.4 = ((bf16[16,128,256]{2,1,0:T(8,128)(2,1)}), bf16[16,128,256]{2,1,0:T(8,128)(2,1)S(1)}, u32[]{:S(2)}, u32[]{:S(2)}) async-start(bf16[16,128,256]{2,1,0:T(8,128)(2,1)} %backward_parts.1), calls=%async_computation.4 | async-start | bytes 2097152 | tf_op jit(solution)/shard_map/all_to_all | solution.py:22
  194.9 26.8 %all-to-all-done.4.parts_ref = bf16[16,128,256]{2,1,0:T(8,128)(2,1)S(1)} async-done(((bf16[16,128,256]{2,1,0:T(8,128)(2,1)}), bf16[16,128,256]{2,1,0:T(8,128)(2,1)S(1)}, u32[]{:S(2)}, u32[]{:S(2)}) %all-to-all-start.4) | async-done | bytes 1048608 | tf_op jit(solution)/shard_map/all_to_all | solution.py:22
  222.6 2.4 masked_total.1
  225.0 32.9 %all_to_all.32.pre_ref = bf16[16,128,256]{2,1,0:T(8,128)(2,1)} all-to-all(bf16[16,128,256]{2,1,0:T(8,128)(2,1)} %masked_total.1), channel_id=1, replica_groups={{0,1,2,3,4,5,6,7,8,9,10,11,12,13,14,15},{16,17,18,19,20,21,22,23,24,25,..., dimensions={0} | all-to-all | bytes 2097152 | tf_op jit(solution)/shard_map/all_to_all | solution.py:22
  257.9 2.5 encoder_grads.1
  (39 shorter events, 14.8 us)
Async XLA Ops:
  0.6 47.1 %copy-start = (s32[1,128,32]{1,2,0:T(8,128)S(1)}, s32[1,128,32]{1,2,0:T(8,128)}, u32[]{:S(2)}) copy-start(s32[1,128,32]{1,2,0:T(8,128)} %param.10) | copy-start | bytes 49156
  4.4 35.8 %all-to-all-start = ((bf16[8,128,512]{2,1,0:T(8,128)(2,1)}), bf16[8,128,512]{2,1,0:T(8,128)(2,1)S(1)}, u32[]{:S(2)}, u32[]{:S(2)}) async-start(bf16[8,128,512]{2,1,0:T(8,128)(2,1)} %pre_parts.1), calls=%async_computation | async-start | bytes 2097152 | tf_op jit(solution)/shard_map/all_to_all | solution.py:22
  13.0 97.0 %copy-start.10 = (bf16[1,128,128]{2,1,0:T(8,128)(2,1)S(1)}, bf16[1,128,128]{2,1,0:T(8,128)(2,1)}, u32[]{:S(2)}) copy-start(bf16[1,128,128]{2,1,0:T(8,128)(2,1)} %param.13) | copy-start | bytes 98308
  17.2 44.5 %collective-permute-start.1 = (bf16[4096,128]{1,0:T(8,128)(2,1)}, bf16[4096,128]{1,0:T(8,128)(2,1)S(1)}, u32[]{:S(2)}, u32[]{:S(2)}) collective-permute-start(bf16[4096,128]{1,0:T(8,128)(2,1)} %get-tuple-element.28), channel_id=1, source_target_pairs={{64,0},{65,1},{66,2},{67,3},{68,4},{69,5},{70,6},{71,7},{72,8},{73... | collective-permute-start | bytes 3145736 | tf_op jit(solution)/shard_map/ppermute | solution.py:39
  18.5 44.5 %collective-permute-start.3 = (bf16[4096,128]{1,0:T(8,128)(2,1)}, bf16[4096,128]{1,0:T(8,128)(2,1)S(1)}, u32[]{:S(2)}, u32[]{:S(2)}) collective-permute-start(bf16[4096,128]{1,0:T(8,128)(2,1)} %get-tuple-element.30), channel_id=1, source_target_pairs={{48,0},{49,1},{50,2},{51,3},{52,4},{53,5},{54,6},{55,7},{56,8},{57... | collective-permute-start | bytes 3145736 | tf_op jit(solution)/shard_map/ppermute | solution.py:39
  19.8 46.2 %collective-permute-start.5 = (bf16[4096,128]{1,0:T(8,128)(2,1)}, bf16[4096,128]{1,0:T(8,128)(2,1)}, u32[]{:S(2)}, u32[]{:S(2)}) collective-permute-start(bf16[4096,128]{1,0:T(8,128)(2,1)} %get-tuple-element.32), channel_id=1, source_target_pairs={{80,0},{81,1},{82,2},{83,3},{84,4},{85,5},{86,6},{87,7},{88,8},{89... | collective-permute-start | bytes 3145736 | tf_op jit(solution)/shard_map/ppermute | solution.py:39
  21.1 69.2 %collective-permute-start.7 = (bf16[4096,128]{1,0:T(8,128)(2,1)}, bf16[4096,128]{1,0:T(8,128)(2,1)}, u32[]{:S(2)}, u32[]{:S(2)}) collective-permute-start(bf16[4096,128]{1,0:T(8,128)(2,1)} %get-tuple-element.37), channel_id=1, source_target_pairs={{112,0},{113,1},{114,2},{115,3},{116,4},{117,5},{118,6},{119,7},{1... | collective-permute-start | bytes 3145736 | tf_op jit(solution)/shard_map/ppermute | solution.py:39
  40.3 1.0 copy-start.6
  43.2 6.7 %collective-permute-start = (bf16[128,512]{1,0:T(8,128)(2,1)}, bf16[128,512]{1,0:T(8,128)(2,1)S(1)}, u32[]{:S(2)}, u32[]{:S(2)}) collective-permute-start(bf16[128,512]{1,0:T(8,128)(2,1)} %part_sum.1.own_ref), channel_id=1, source_target_pairs={{0,8},{1,9},{2,10},{3,11},{4,12},{5,13},{6,14},{7,15},{8,0},{9,1},... | collective-permute-start | bytes 393224 | tf_op jit(solution)/shard_map/ppermute | solution.py:44
  49.9 0.7 copy-start.8
  52.7 62.2 %all-to-all-start.1 = ((bf16[8,128,512]{2,1,0:T(8,128)(2,1)}), bf16[8,128,512]{2,1,0:T(8,128)(2,1)S(1)}, u32[]{:S(2)}, u32[]{:S(2)}) async-start(bf16[8,128,512]{2,1,0:T(8,128)(2,1)} %masked_sum.1), calls=%async_computation.1 | async-start | bytes 2097152 | tf_op jit(solution)/shard_map/all_to_all | solution.py:22
  61.7 53.2 %collective-permute-start.2 = (bf16[4096,128]{1,0:T(8,128)(2,1)}, bf16[4096,128]{1,0:T(8,128)(2,1)}, u32[]{:S(2)}, u32[]{:S(2)}) collective-permute-start(bf16[4096,128]{1,0:T(8,128)(2,1)} %get-tuple-element.29), channel_id=1, source_target_pairs={{32,0},{33,1},{34,2},{35,3},{36,4},{37,5},{38,6},{39,7},{40,8},{41... | collective-permute-start | bytes 3145736 | tf_op jit(solution)/shard_map/ppermute | solution.py:39
  63.0 51.9 %collective-permute-start.4 = (bf16[4096,128]{1,0:T(8,128)(2,1)}, bf16[4096,128]{1,0:T(8,128)(2,1)}, u32[]{:S(2)}, u32[]{:S(2)}) collective-permute-start(bf16[4096,128]{1,0:T(8,128)(2,1)} %get-tuple-element.31), channel_id=1, source_target_pairs={{96,0},{97,1},{98,2},{99,3},{100,4},{101,5},{102,6},{103,7},{104,8... | collective-permute-start | bytes 3145736 | tf_op jit(solution)/shard_map/ppermute | solution.py:39
  66.1 48.8 %collective-permute-start.6 = (bf16[4096,128]{1,0:T(8,128)(2,1)}, bf16[4096,128]{1,0:T(8,128)(2,1)}, u32[]{:S(2)}, u32[]{:S(2)}) collective-permute-start(bf16[4096,128]{1,0:T(8,128)(2,1)} %get-tuple-element.33), channel_id=1, source_target_pairs={{16,0},{17,1},{18,2},{19,3},{20,4},{21,5},{22,6},{23,7},{24,8},{25... | collective-permute-start | bytes 3145736 | tf_op jit(solution)/shard_map/ppermute | solution.py:39
  90.3 18.9 %collective-permute-start.8 = (bf16[2048,128]{1,0:T(8,128)(2,1)}, bf16[2048,128]{1,0:T(8,128)(2,1)S(1)}, u32[]{:S(2)}, u32[]{:S(2)}) collective-permute-start(bf16[2048,128]{1,0:T(8,128)(2,1)} %bitcast.24), channel_id=1, source_target_pairs={{128,0},{129,1},{130,2},{131,3},{132,4},{133,5},{134,6},{135,7},{1... | collective-permute-start | bytes 1572872 | tf_op jit(solution)/shard_map/ppermute | solution.py:39
  109.2 0.8 copy-start.3
  110.0 13.7 %collective-permute-start.9 = (bf16[128,128]{1,0:T(8,128)(2,1)S(1)}, bf16[128,128]{1,0:T(8,128)(2,1)S(1)}, u32[]{:S(2)}, u32[]{:S(2)}) collective-permute-start(bf16[128,128]{1,0:T(8,128)(2,1)S(1)} %bitcast.36), channel_id=1, source_target_pairs={{0,8},{1,9},{2,10},{3,11},{4,12},{5,13},{6,14},{7,15},{8,0},{9,1},... | collective-permute-start | bytes 98312 | tf_op jit(solution)/shard_map/ppermute | solution.py:44
  114.9 1.0 copy-start.1
  116.0 1.0 copy-start.4
  123.7 34.2 %copy-start.11 = (bf16[128,128]{1,0:T(8,128)(2,1)}, bf16[128,128]{1,0:T(8,128)(2,1)S(1)}, u32[]{:S(2)}) copy-start(bf16[128,128]{1,0:T(8,128)(2,1)S(1)} %collective-permute-done.9.away_target_ref) | copy-start | bytes 98308
  152.0 6.0 %collective-permute-start.10 = (bf16[2,128,128]{2,1,0:T(8,128)(2,1)}, bf16[2,128,128]{2,1,0:T(8,128)(2,1)S(1)}, u32[]{:S(2)}, u32[]{:S(2)}) collective-permute-start(bf16[2,128,128]{2,1,0:T(8,128)(2,1)} %get-tuple-element.45), channel_id=1, source_target_pairs={{0,8},{1,9},{2,10},{3,11},{4,12},{5,13},{6,14},{7,15},{8,0},{9,1},... | collective-permute-start | bytes 196616 | tf_op jit(solution)/shard_map/ppermute | solution.py:44
  157.9 0.6 copy-start.9
  174.7 1.0 copy-start.2
  175.8 1.0 copy-start.5
  186.2 35.5 %all-to-all-start.4 = ((bf16[16,128,256]{2,1,0:T(8,128)(2,1)}), bf16[16,128,256]{2,1,0:T(8,128)(2,1)S(1)}, u32[]{:S(2)}, u32[]{:S(2)}) async-start(bf16[16,128,256]{2,1,0:T(8,128)(2,1)} %backward_parts.1), calls=%async_computation.4 | async-start | bytes 2097152 | tf_op jit(solution)/shard_map/all_to_all | solution.py:22
  221.7 1.0 copy-start.7

commit v5 on v4

--- a/solution.py
+++ b/solution.py
@@ -176,7 +176,7 @@
             out_ref[lax.rem(place + r, layers)] = kept.astype(BF16)
 
 
-def forward_shares(place, acts, near, far, moved, chunk=1024):
+def forward_shares(place, acts, near, far, moved, chunk=2048):
     slots, features, cols = near.shape
     parts, tokens, columns = acts.shape
     layers = 2 * slots
@@ -280,7 +280,7 @@
         out_ref[part] = product[:, part * columns : (part + 1) * columns].astype(BF16)
 
 
-def backward_parts(place, grads, near, far, moved, parts, chunk=1024):
+def backward_parts(place, grads, near, far, moved, parts, chunk=2048):
     slots, features, cols = near.shape
     layers, tokens, _ = grads.shape
     columns = features // parts

time: 262 us -> 261 us (level)
  no operation moved by 1% of the time
where the time goes in v5:
time: 261 us; the launch traced here: 260 us
  waiting for transfers between devices  93 us (36%)
  blocking collectives  73.7 us (28%)
  starting transfers between devices  41.6 us (16%)
  Pallas kernels  32.2 us (12%)
  local copies, waits for them, and re-layouts  18.8 us (7%)
    all_to_all x3, blocking collectives, exchange(): lax.all_to_all(parts, axis, 0, 0, tiled=True, axis_index_groups=groups)  73.7 us
    all_to_all x3, waiting for transfers between devices, exchange(): lax.all_to_all(parts, axis, 0, 0, tiled=True, axis_index_groups=groups)  44.5 us
    ppermute x8, waiting for transfers between devices, shifted_down(): return lax.ppermute(block, ('blk', 'width'), route)  42.3 us
    all_to_all x3, starting transfers between devices, exchange(): lax.all_to_all(parts, axis, 0, 0, tiled=True, axis_index_groups=groups)  21.9 us
    ppermute x8, starting transfers between devices, shifted_down(): return lax.ppermute(block, ('blk', 'width'), route)  10.3 us
    pallas_call x1, Pallas kernels, backward_parts(): pl.pallas_call(functools.partial(backward_kernel, far.shape[0] // chunk),...  9.56 us
    ppermute x3, starting transfers between devices, other_half(): lax.ppermute(block, 'width', [(p, (p + parts // 2) % parts) for p in rang...  9.41 us
    unnamed x24, local copies, waits for them, and re-layouts  8.18 us
  transfers between devices with their start and end apart: 14, of which 7 were waited for; matrix products, arithmetic and copies ran while one was open for 4% of the time, Pallas kernels for 4%

profile of v5, /device:TPU:32, one launch (start us, length us, event | category | flops | bytes accessed | tf_op | source)
XLA Modules:
  0.0 260.2 jit_solution(11579220423642021949)
XLA Ops:
  0.6 3.8 %pre_parts.1 = bf16[8,128,512]{2,1,0:T(8,128)(2,1)} custom-call(bf16[128,128]{1,0:T(8,128)(2,1)} %bitcast.33, bf16[128,4096]{1,0:T(8,128)(2,1)} %bitcast.30), custom_call_target="tpu_custom_call" | custom-call | tf_op jit(solution)/shard_map/pre_parts/pallas_call | solution.py:59
  4.4 8.6 %all-to-all-start = ((bf16[8,128,512]{2,1,0:T(8,128)(2,1)}), bf16[8,128,512]{2,1,0:T(8,128)(2,1)S(1)}, u32[]{:S(2)}, u32[]{:S(2)}) async-start(bf16[8,128,512]{2,1,0:T(8,128)(2,1)} %pre_parts.1), calls=%async_computation | async-start | bytes 2097152 | tf_op jit(solution)/shard_map/all_to_all | solution.py:22
  13.0 4.3 %slice_bitcast_fusion.3 = (bf16[4096,128]{1,0:T(8,128)(2,1)}, bf16[4096,128]{1,0:T(8,128)(2,1)}, bf16[4096,128]{1,0:T(8,128)(2,1)}, bf16[4096,128]{1,0:T(8,128)(2,1)}) fusion(bf16[1,8,4096,128]{3,2,1,0:T(8,128)(2,1)} %param.11), kind=kLoop, calls=%fused_computation.3 | loop fusion | bytes 8388608 | tf_op jit(solution)/shard_map/squeeze | solution.py:353
  18.5 1.3 collective-permute-start.3
  19.8 1.3 collective-permute-start.5
  21.1 1.3 collective-permute-start.7
  22.5 17.8 %all-to-all-done.parts_ref = bf16[8,128,512]{2,1,0:T(8,128)(2,1)S(1)} async-done(((bf16[8,128,512]{2,1,0:T(8,128)(2,1)}), bf16[8,128,512]{2,1,0:T(8,128)(2,1)S(1)}, u32[]{:S(2)}, u32[]{:S(2)}) %all-to-all-start) | async-done | bytes 1048608 | tf_op jit(solution)/shard_map/all_to_all | solution.py:22
  41.2 2.0 part_sum.1.own_ref
  43.2 3.2 %collective-permute-start = (bf16[128,512]{1,0:T(8,128)(2,1)}, bf16[128,512]{1,0:T(8,128)(2,1)S(1)}, u32[]{:S(2)}, u32[]{:S(2)}) collective-permute-start(bf16[128,512]{1,0:T(8,128)(2,1)} %part_sum.1.own_ref), channel_id=1, source_target_pairs={{0,8},{1,9},{2,10},{3,11},{4,12},{5,13},{6,14},{7,15},{8,0},{9,1},... | collective-permute-start | bytes 393224 | tf_op jit(solution)/shard_map/ppermute | solution.py:44
  48.4 1.5 collective-permute-done.came_ref
  50.6 2.1 masked_sum.1
  52.7 5.4 %all-to-all-start.1 = ((bf16[8,128,512]{2,1,0:T(8,128)(2,1)}), bf16[8,128,512]{2,1,0:T(8,128)(2,1)S(1)}, u32[]{:S(2)}, u32[]{:S(2)}) async-start(bf16[8,128,512]{2,1,0:T(8,128)(2,1)} %masked_sum.1), calls=%async_computation.1 | async-start | bytes 2097152 | tf_op jit(solution)/shard_map/all_to_all | solution.py:22
  58.1 3.6 %slice_bitcast_fusion = (bf16[4096,128]{1,0:T(8,128)(2,1)}, bf16[4096,128]{1,0:T(8,128)(2,1)}, bf16[4096,128]{1,0:T(8,128)(2,1)}) fusion(bf16[8,4096,128]{2,1,0:T(8,128)(2,1)} %bitcast.27), kind=kLoop, calls=%fused_computation | loop fusion | bytes 6291456 | tf_op jit(solution)/shard_map/squeeze | solution.py:367
  61.7 1.3 collective-permute-start.2
  63.0 1.3 collective-permute-start.4
  64.3 1.8 collective-permute-done.5.refs_5_
  67.4 22.9 %collective-permute-done.7.refs_6_ = bf16[4096,128]{1,0:T(8,128)(2,1)} collective-permute-done((bf16[4096,128]{1,0:T(8,128)(2,1)}, bf16[4096,128]{1,0:T(8,128)(2,1)}, u32[]{:S(2)}, u32[]{:S(2)}) %collective-permute-start.7) | collective-permute-done | bytes 1048608 | tf_op jit(solution)/shard_map/ppermute | solution.py:39
  91.6 17.6 %collective-permute-done.8.refs_7_ = bf16[2048,128]{1,0:T(8,128)(2,1)S(1)} collective-permute-done((bf16[2048,128]{1,0:T(8,128)(2,1)}, bf16[2048,128]{1,0:T(8,128)(2,1)S(1)}, u32[]{:S(2)}, u32[]{:S(2)}) %collective-permute-start.8) | collective-permute-done | bytes 524320 | tf_op jit(solution)/shard_map/ppermute | solution.py:39
  110.0 4.9 %collective-permute-start.9 = (bf16[128,128]{1,0:T(8,128)(2,1)S(1)}, bf16[128,128]{1,0:T(8,128)(2,1)S(1)}, u32[]{:S(2)}, u32[]{:S(2)}) collective-permute-start(bf16[128,128]{1,0:T(8,128)(2,1)S(1)} %bitcast.36), channel_id=1, source_target_pairs={{0,8},{1,9},{2,10},{3,11},{4,12},{5,13},{6,14},{7,15},{8,0},{9,1},... | collective-permute-start | bytes 98312 | tf_op jit(solution)/shard_map/ppermute | solution.py:44
  117.0 6.2 %forward_shares.1 = bf16[16,128,128]{2,1,0:T(8,128)(2,1)S(1)} custom-call(s32[1]{0:T(128)} %bitcast.place_ref, bf16[8,128,512]{2,1,0:T(8,128)(2,1)S(1)} %all-to-all-done.1.acts_ref, bf16[8,4096,128]{2,1,0:T(8,128)(2,1)} %bitcast.28, bf16[2048,128]{1,0:T(8,128)(2,1)S(1)} %bitcast.25, bf16[4096,128]{1,0:T(8,128)(2,1)} %collective-permute-done.2.refs_0_, ...), custom_call_target="tpu_custom_call" | custom-call | tf_op jit(solution)/shard_map/forward_shares/pallas_call | solution.py:183
  123.3 26.4 %all_to_all.30.shares_ref = bf16[16,128,128]{2,1,0:T(8,128)(2,1)} all-to-all(bf16[16,128,128]{2,1,0:T(8,128)(2,1)S(1)} %forward_shares.1), channel_id=1, replica_groups={{0,16,32,48,64,80,96,112,128,144,160,176,192,208,224,240},{1,17,33,49,6..., dimensions={0} | all-to-all | bytes 1048576 | tf_op jit(solution)/shard_map/all_to_all | solution.py:22
  149.7 1.8 share_sums.1
  151.5 1.3 collective-permute-start.10
  152.9 4.7 %collective-permute-done.10.came_ref = bf16[2,128,128]{2,1,0:T(8,128)(2,1)S(1)} collective-permute-done((bf16[2,128,128]{2,1,0:T(8,128)(2,1)}, bf16[2,128,128]{2,1,0:T(8,128)(2,1)S(1)}, u32[]{:S(2)}, u32[]{:S(2)}) %collective-permute-start.10) | collective-permute-done | bytes 65568 | tf_op jit(solution)/shard_map/ppermute | solution.py:44
  158.1 1.8 residual.1
  159.9 14.4 %all_to_all.31.grads_ref = bf16[16,128,128]{2,1,0:T(8,128)(2,1)S(1)} all-to-all(bf16[16,128,128]{2,1,0:T(8,128)(2,1)} %get-tuple-element.48), channel_id=1, replica_groups={{0,16,32,48,64,80,96,112,128,144,160,176,192,208,224,240},{1,17,33,49,6..., dimensions={0} | all-to-all | bytes 1048576 | tf_op jit(solution)/shard_map/all_to_all | solution.py:22
  176.4 9.6 %backward_parts.1 = bf16[16,128,256]{2,1,0:T(8,128)(2,1)} custom-call(s32[1]{0:T(128)} %bitcast.place_ref, bf16[16,128,128]{2,1,0:T(8,128)(2,1)S(1)} %all_to_all.31.grads_ref, bf16[8,4096,128]{2,1,0:T(8,128)(2,1)} %bitcast.29, bf16[2048,128]{1,0:T(8,128)(2,1)S(1)} %bitcast.26, bf16[4096,128]{1,0:T(8,128)(2,1)} %collective-permute-done.2.refs_0_, ...), custom_call_target="tpu_custom_call" | custom-call | tf_op jit(solution)/shard_map/backward_parts/pallas_call | solution.py:287
  185.9 8.0 %all-to-all-start.4 = ((bf16[16,128,256]{2,1,0:T(8,128)(2,1)}), bf16[16,128,256]{2,1,0:T(8,128)(2,1)S(1)}, u32[]{:S(2)}, u32[]{:S(2)}) async-start(bf16[16,128,256]{2,1,0:T(8,128)(2,1)} %backward_parts.1), calls=%async_computation.4 | async-start | bytes 2097152 | tf_op jit(solution)/shard_map/all_to_all | solution.py:22
  194.7 26.7 %all-to-all-done.4.parts_ref = bf16[16,128,256]{2,1,0:T(8,128)(2,1)S(1)} async-done(((bf16[16,128,256]{2,1,0:T(8,128)(2,1)}), bf16[16,128,256]{2,1,0:T(8,128)(2,1)S(1)}, u32[]{:S(2)}, u32[]{:S(2)}) %all-to-all-start.4) | async-done | bytes 1048608 | tf_op jit(solution)/shard_map/all_to_all | solution.py:22
  222.4 2.4 masked_total.1
  224.8 32.9 %all_to_all.32.pre_ref = bf16[16,128,256]{2,1,0:T(8,128)(2,1)} all-to-all(bf16[16,128,256]{2,1,0:T(8,128)(2,1)} %masked_total.1), channel_id=1, replica_groups={{0,1,2,3,4,5,6,7,8,9,10,11,12,13,14,15},{16,17,18,19,20,21,22,23,24,25,..., dimensions={0} | all-to-all | bytes 2097152 | tf_op jit(solution)/shard_map/all_to_all | solution.py:22
  257.7 2.5 encoder_grads.1
  (39 shorter events, 14.8 us)
Async XLA Ops:
  0.6 47.1 %copy-start = (s32[1,128,32]{1,2,0:T(8,128)S(1)}, s32[1,128,32]{1,2,0:T(8,128)}, u32[]{:S(2)}) copy-start(s32[1,128,32]{1,2,0:T(8,128)} %param.10) | copy-start | bytes 49156
  4.4 35.8 %all-to-all-start = ((bf16[8,128,512]{2,1,0:T(8,128)(2,1)}), bf16[8,128,512]{2,1,0:T(8,128)(2,1)S(1)}, u32[]{:S(2)}, u32[]{:S(2)}) async-start(bf16[8,128,512]{2,1,0:T(8,128)(2,1)} %pre_parts.1), calls=%async_computation | async-start | bytes 2097152 | tf_op jit(solution)/shard_map/all_to_all | solution.py:22
  13.0 97.0 %copy-start.10 = (bf16[1,128,128]{2,1,0:T(8,128)(2,1)S(1)}, bf16[1,128,128]{2,1,0:T(8,128)(2,1)}, u32[]{:S(2)}) copy-start(bf16[1,128,128]{2,1,0:T(8,128)(2,1)} %param.13) | copy-start | bytes 98308
  17.2 44.5 %collective-permute-start.1 = (bf16[4096,128]{1,0:T(8,128)(2,1)}, bf16[4096,128]{1,0:T(8,128)(2,1)S(1)}, u32[]{:S(2)}, u32[]{:S(2)}) collective-permute-start(bf16[4096,128]{1,0:T(8,128)(2,1)} %get-tuple-element.28), channel_id=1, source_target_pairs={{64,0},{65,1},{66,2},{67,3},{68,4},{69,5},{70,6},{71,7},{72,8},{73... | collective-permute-start | bytes 3145736 | tf_op jit(solution)/shard_map/ppermute | solution.py:39
  18.5 44.5 %collective-permute-start.3 = (bf16[4096,128]{1,0:T(8,128)(2,1)}, bf16[4096,128]{1,0:T(8,128)(2,1)S(1)}, u32[]{:S(2)}, u32[]{:S(2)}) collective-permute-start(bf16[4096,128]{1,0:T(8,128)(2,1)} %get-tuple-element.30), channel_id=1, source_target_pairs={{48,0},{49,1},{50,2},{51,3},{52,4},{53,5},{54,6},{55,7},{56,8},{57... | collective-permute-start | bytes 3145736 | tf_op jit(solution)/shard_map/ppermute | solution.py:39
  19.8 46.2 %collective-permute-start.5 = (bf16[4096,128]{1,0:T(8,128)(2,1)}, bf16[4096,128]{1,0:T(8,128)(2,1)}, u32[]{:S(2)}, u32[]{:S(2)}) collective-permute-start(bf16[4096,128]{1,0:T(8,128)(2,1)} %get-tuple-element.32), channel_id=1, source_target_pairs={{80,0},{81,1},{82,2},{83,3},{84,4},{85,5},{86,6},{87,7},{88,8},{89... | collective-permute-start | bytes 3145736 | tf_op jit(solution)/shard_map/ppermute | solution.py:39
  21.1 69.2 %collective-permute-start.7 = (bf16[4096,128]{1,0:T(8,128)(2,1)}, bf16[4096,128]{1,0:T(8,128)(2,1)}, u32[]{:S(2)}, u32[]{:S(2)}) collective-permute-start(bf16[4096,128]{1,0:T(8,128)(2,1)} %get-tuple-element.37), channel_id=1, source_target_pairs={{112,0},{113,1},{114,2},{115,3},{116,4},{117,5},{118,6},{119,7},{1... | collective-permute-start | bytes 3145736 | tf_op jit(solution)/shard_map/ppermute | solution.py:39
  40.3 1.0 copy-start.6
  43.2 6.7 %collective-permute-start = (bf16[128,512]{1,0:T(8,128)(2,1)}, bf16[128,512]{1,0:T(8,128)(2,1)S(1)}, u32[]{:S(2)}, u32[]{:S(2)}) collective-permute-start(bf16[128,512]{1,0:T(8,128)(2,1)} %part_sum.1.own_ref), channel_id=1, source_target_pairs={{0,8},{1,9},{2,10},{3,11},{4,12},{5,13},{6,14},{7,15},{8,0},{9,1},... | collective-permute-start | bytes 393224 | tf_op jit(solution)/shard_map/ppermute | solution.py:44
  49.9 0.7 copy-start.8
  52.7 62.2 %all-to-all-start.1 = ((bf16[8,128,512]{2,1,0:T(8,128)(2,1)}), bf16[8,128,512]{2,1,0:T(8,128)(2,1)S(1)}, u32[]{:S(2)}, u32[]{:S(2)}) async-start(bf16[8,128,512]{2,1,0:T(8,128)(2,1)} %masked_sum.1), calls=%async_computation.1 | async-start | bytes 2097152 | tf_op jit(solution)/shard_map/all_to_all | solution.py:22
  61.7 53.2 %collective-permute-start.2 = (bf16[4096,128]{1,0:T(8,128)(2,1)}, bf16[4096,128]{1,0:T(8,128)(2,1)}, u32[]{:S(2)}, u32[]{:S(2)}) collective-permute-start(bf16[4096,128]{1,0:T(8,128)(2,1)} %get-tuple-element.29), channel_id=1, source_target_pairs={{32,0},{33,1},{34,2},{35,3},{36,4},{37,5},{38,6},{39,7},{40,8},{41... | collective-permute-start | bytes 3145736 | tf_op jit(solution)/shard_map/ppermute | solution.py:39
  63.0 51.9 %collective-permute-start.4 = (bf16[4096,128]{1,0:T(8,128)(2,1)}, bf16[4096,128]{1,0:T(8,128)(2,1)}, u32[]{:S(2)}, u32[]{:S(2)}) collective-permute-start(bf16[4096,128]{1,0:T(8,128)(2,1)} %get-tuple-element.31), channel_id=1, source_target_pairs={{96,0},{97,1},{98,2},{99,3},{100,4},{101,5},{102,6},{103,7},{104,8... | collective-permute-start | bytes 3145736 | tf_op jit(solution)/shard_map/ppermute | solution.py:39
  66.1 48.8 %collective-permute-start.6 = (bf16[4096,128]{1,0:T(8,128)(2,1)}, bf16[4096,128]{1,0:T(8,128)(2,1)}, u32[]{:S(2)}, u32[]{:S(2)}) collective-permute-start(bf16[4096,128]{1,0:T(8,128)(2,1)} %get-tuple-element.33), channel_id=1, source_target_pairs={{16,0},{17,1},{18,2},{19,3},{20,4},{21,5},{22,6},{23,7},{24,8},{25... | collective-permute-start | bytes 3145736 | tf_op jit(solution)/shard_map/ppermute | solution.py:39
  90.3 18.9 %collective-permute-start.8 = (bf16[2048,128]{1,0:T(8,128)(2,1)}, bf16[2048,128]{1,0:T(8,128)(2,1)S(1)}, u32[]{:S(2)}, u32[]{:S(2)}) collective-permute-start(bf16[2048,128]{1,0:T(8,128)(2,1)} %bitcast.24), channel_id=1, source_target_pairs={{128,0},{129,1},{130,2},{131,3},{132,4},{133,5},{134,6},{135,7},{1... | collective-permute-start | bytes 1572872 | tf_op jit(solution)/shard_map/ppermute | solution.py:39
  109.2 0.8 copy-start.3
  110.0 13.2 %collective-permute-start.9 = (bf16[128,128]{1,0:T(8,128)(2,1)S(1)}, bf16[128,128]{1,0:T(8,128)(2,1)S(1)}, u32[]{:S(2)}, u32[]{:S(2)}) collective-permute-start(bf16[128,128]{1,0:T(8,128)(2,1)S(1)} %bitcast.36), channel_id=1, source_target_pairs={{0,8},{1,9},{2,10},{3,11},{4,12},{5,13},{6,14},{7,15},{8,0},{9,1},... | collective-permute-start | bytes 98312 | tf_op jit(solution)/shard_map/ppermute | solution.py:44
  114.9 1.0 copy-start.1
  116.0 1.0 copy-start.4
  123.3 34.2 %copy-start.11 = (bf16[128,128]{1,0:T(8,128)(2,1)}, bf16[128,128]{1,0:T(8,128)(2,1)S(1)}, u32[]{:S(2)}) copy-start(bf16[128,128]{1,0:T(8,128)(2,1)S(1)} %collective-permute-done.9.away_target_ref) | copy-start | bytes 98308
  151.5 6.0 %collective-permute-start.10 = (bf16[2,128,128]{2,1,0:T(8,128)(2,1)}, bf16[2,128,128]{2,1,0:T(8,128)(2,1)S(1)}, u32[]{:S(2)}, u32[]{:S(2)}) collective-permute-start(bf16[2,128,128]{2,1,0:T(8,128)(2,1)} %get-tuple-element.45), channel_id=1, source_target_pairs={{0,8},{1,9},{2,10},{3,11},{4,12},{5,13},{6,14},{7,15},{8,0},{9,1},... | collective-permute-start | bytes 196616 | tf_op jit(solution)/shard_map/ppermute | solution.py:44
  157.5 0.6 copy-start.9
  174.3 1.0 copy-start.2
  175.3 1.0 copy-start.5
  185.9 35.5 %all-to-all-start.4 = ((bf16[16,128,256]{2,1,0:T(8,128)(2,1)}), bf16[16,128,256]{2,1,0:T(8,128)(2,1)S(1)}, u32[]{:S(2)}, u32[]{:S(2)}) async-start(bf16[16,128,256]{2,1,0:T(8,128)(2,1)} %backward_parts.1), calls=%async_computation.4 | async-start | bytes 2097152 | tf_op jit(solution)/shard_map/all_to_all | solution.py:22
  221.4 1.0 copy-start.7
